TPU v7x, 32 devices: a whole 2x2x4 slice. The times are simulated.
32 devices in a mesh: dp: 8 (over z, y), rep: 4 (over x, core).
Axes of the slice: x: 2, y: 2, z: 4, core: 2. Of those that a mesh axis runs over, the one named last changes fastest.
Arguments:
- tokens: bfloat16 [4096, 768], P(('dp', 'rep')), may hold values from -6 to 6
- seq_lengths: int32 [8, 3], P('dp'), may hold values from 0 to 512, as said below
- bucket_ids: int32 [1023], replicated, may hold values from 0 to 31
- routes: int32 [4096, 1], P(('dp', 'rep')), may hold values from 0 to 7; in each aligned block of 128 rows (0 to 127, 128 to 255, ...) at most 18 rows name the same one
- norm1_gain: bfloat16 [768], P('dp'), may hold values from 0.5 to 1.5
- w_query: bfloat16 [768, 768], P('dp'), may hold values from -0.21875 to 0.21875
- w_key: bfloat16 [768, 768], P('dp'), may hold values from -0.21875 to 0.21875
- w_value: bfloat16 [768, 768], P('dp'), may hold values from -0.21875 to 0.21875
- w_output: bfloat16 [768, 768], P('dp'), may hold values from -2.5 to 2.5
- rel_bias: bfloat16 [384], P('dp'), may hold values from -3 to 3
- norm2_gain: bfloat16 [768], P('dp'), may hold values from 0.5 to 1.5
- w_router: bfloat16 [768, 8], P('dp'), may hold values from -0.15625 to 0.15625
- w_in: bfloat16 [768, 24576], P(None, 'dp'), may hold values from -0.21875 to 0.21875
- w_out: bfloat16 [24576, 768], P('dp'), may hold values from -0.875 to 0.875
- cotangent: bfloat16 [4096, 768], P(('dp', 'rep')), may hold values from -6 to 6
Outputs:
- block_out: bfloat16 [4096, 768], P(('dp', 'rep'))
- grad_input: float32 [4096, 768], P(('dp', 'rep'))
- grad_norm1: float32 [768], P('dp')
- grad_query: float32 [768, 768], P('dp')
- grad_key: float32 [768, 768], P('dp')
- grad_value: float32 [768, 768], P('dp')
- grad_output: float32 [768, 768], P('dp')
- grad_rel_bias: float32 [384], P('dp')
- grad_norm2: float32 [768], P('dp')
- grad_router: float32 [768, 8], P('dp')
- grad_w_in: float32 [768, 24576], P(None, 'dp')
- grad_w_out: float32 [24576, 768], P('dp')
Inputs may be any that keep to these rules, and one draw needn't show every extreme that they name: `seq_lengths`: row g lists the lengths of group g's sequences in order, then zeros; one to 3 are nonzero and they sum to at most 512. One sequence of each group starts in its first 128 places and ends in its last 128. `routes`: among one device's 128 tokens at most 18 name the same expert.
All inputs are finite; a program needn't handle non-finite values.
Results may differ from a plain program's by a relative error of at most 0.018.
Values may be sent and summed in bfloat16 or wider, within the bound.
A program may use at most 192 MiB of HBM per device.

v0:
```python
import jax
import jax.numpy as jnp
from jax import lax
from jax.sharding import PartitionSpec as P

HEADS = 12
HEAD = 64
BUCKETS = 32
EXPERTS = 8


EPS = 1e-06
NEG = -1e30
HIGH = lax.Precision.HIGHEST


def rms_scale(rows_in, gain_vec):
    return rows_in * lax.rsqrt(jnp.mean(rows_in * rows_in, axis=-1, keepdims=True) + EPS) * gain_vec


def matmul(left_op, right_op):
    return jnp.dot(left_op, right_op, preferred_element_type=jnp.float32)


def bias_block(bias_flat, bucket_ids, first_row, row_count, group_rows):
    bias_grid = bias_flat.reshape(HEADS, BUCKETS)
    bucket_onehot = (bucket_ids[None, :] == jnp.arange(BUCKETS, dtype=jnp.int32)[:, None]).astype(
        jnp.float32
    )
    by_offset = jnp.dot(bias_grid, bucket_onehot, precision=HIGH)
    query_at = first_row + jnp.arange(row_count, dtype=jnp.int32)
    offsets = (
        query_at[:, None] - jnp.arange(group_rows, dtype=jnp.int32)[None, :] + (group_rows - 1)
    )
    return by_offset[:, offsets]


def masked_scores(q_heads, k_heads, rel_terms, allowed):
    raw_scores = jnp.einsum(
        "qhd,khd->hqk", q_heads, k_heads, preferred_element_type=jnp.float32
    ) * HEAD ** (-0.5)
    return jnp.where(allowed[None], raw_scores + rel_terms, NEG)


def on_device(
    tokens,
    seq_lengths,
    bucket_ids,
    routes,
    norm1_gain,
    w_query,
    w_key,
    w_value,
    w_output,
    rel_bias,
    norm2_gain,
    w_router,
    w_in,
    w_out,
    cotangent,
):
    row_count, model_width = tokens.shape
    group_rows = row_count * lax.axis_size("rep")
    first_row = lax.axis_index("rep") * row_count
    split_count = lax.axis_size("dp") // EXPERTS
    capacity = row_count // 8 + row_count // 64
    gathered = (
        lax.all_gather(norm1_gain, "dp", axis=0, tiled=True),
        lax.all_gather(w_query, "dp", axis=0, tiled=True),
        lax.all_gather(w_key, "dp", axis=0, tiled=True),
        lax.all_gather(w_value, "dp", axis=0, tiled=True),
        lax.all_gather(w_output, "dp", axis=0, tiled=True),
        lax.all_gather(rel_bias, "dp", axis=0, tiled=True),
        lax.all_gather(norm2_gain, "dp", axis=0, tiled=True),
        lax.all_gather(w_router, "dp", axis=0, tiled=True),
    )
    gain_one, query_full, key_full, value_full, output_full, table_full, gain_two, router_full = (
        gathered
    )
    seq_ends = jnp.cumsum(seq_lengths[0])
    places = jnp.arange(group_rows, dtype=jnp.int32)
    segment = jnp.sum((places[:, None] >= seq_ends[None, :]).astype(jnp.int32), axis=1)
    own_segment = lax.dynamic_slice_in_dim(segment, first_row, row_count)
    allowed = own_segment[:, None] == segment[None, :]
    live_bool = first_row + jnp.arange(row_count, dtype=jnp.int32) < seq_ends[-1]
    row_live = live_bool.astype(jnp.float32)[:, None]
    x_in = tokens.astype(jnp.float32)
    gain_first = gain_one.astype(jnp.float32)
    h_one = rms_scale(x_in, gain_first).astype(jnp.bfloat16)
    q_low = matmul(h_one, query_full).astype(jnp.bfloat16)
    k_low = matmul(h_one, key_full).astype(jnp.bfloat16)
    v_low = matmul(h_one, value_full).astype(jnp.bfloat16)
    k_group, v_group = (
        lax.all_gather(k_low, "rep", axis=0, tiled=True),
        lax.all_gather(v_low, "rep", axis=0, tiled=True),
    )
    q_heads = q_low.reshape(row_count, HEADS, HEAD)
    k_heads = k_group.reshape(group_rows, HEADS, HEAD)
    v_heads = v_group.reshape(group_rows, HEADS, HEAD)
    table_float = table_full.astype(jnp.float32)
    rel_terms = bias_block(table_float, bucket_ids, first_row, row_count, group_rows)
    scores = masked_scores(q_heads, k_heads, rel_terms, allowed)
    row_max = jnp.max(scores, axis=-1, keepdims=True)
    log_total = row_max + jnp.log(jnp.sum(jnp.exp(scores - row_max), axis=-1, keepdims=True))
    attend_probs = jnp.exp(scores - log_total).astype(jnp.bfloat16)
    mixture = jnp.einsum("hqk,khd->qhd", attend_probs, v_heads, preferred_element_type=jnp.float32)
    mixture = mixture.reshape(row_count, model_width).astype(jnp.bfloat16)
    branch = matmul(mixture, output_full)
    x_one = x_in + row_live * branch
    gain_second = gain_two.astype(jnp.float32)
    h_two = rms_scale(x_one, gain_second).astype(jnp.bfloat16)
    router_probs = jax.nn.softmax(matmul(h_two, router_full), axis=-1)
    route_ids = routes[:, 0]
    route_onehot = route_ids[:, None] == jnp.arange(EXPERTS, dtype=jnp.int32)[None, :]
    gate_vals = jnp.sum(router_probs * route_onehot.astype(jnp.float32), axis=1, keepdims=True)
    chosen = route_onehot & live_bool[:, None]
    counts = jnp.cumsum(chosen.astype(jnp.int32), axis=0)
    rank_in = jnp.sum(jnp.where(chosen, counts - 1, 0), axis=1)
    slot_ids = jnp.where(live_bool, route_ids * capacity + rank_in, -1)
    slot_safe = jnp.maximum(slot_ids, 0)
    dispatch = (
        jnp.arange(EXPERTS * capacity, dtype=jnp.int32)[:, None] == slot_ids[None, :]
    ).astype(jnp.bfloat16)

    def spread(slot_rows):
        widened = jnp.broadcast_to(
            slot_rows.reshape(EXPERTS, 1, capacity, model_width),
            (EXPERTS, split_count, capacity, model_width),
        )
        return widened.reshape(EXPERTS * split_count, capacity, model_width)

    def collect(returned):
        stacked = returned.astype(jnp.float32).reshape(EXPERTS, split_count, capacity, model_width)
        return jnp.sum(stacked, axis=1).reshape(EXPERTS * capacity, model_width)

    send_rows = spread(matmul(dispatch, h_two).astype(jnp.bfloat16))
    recv_rows = lax.all_to_all(send_rows, "dp", split_axis=0, concat_axis=0, tiled=True).reshape(
        -1, model_width
    )
    hidden_pre = matmul(recv_rows, w_in)
    activation = jax.nn.gelu(hidden_pre, approximate=True).astype(jnp.bfloat16)
    partial_value = (
        matmul(activation, w_out).astype(jnp.bfloat16).reshape(-1, capacity, model_width)
    )
    returned = lax.all_to_all(partial_value, "dp", split_axis=0, concat_axis=0, tiled=True)
    expert_rows = jnp.take(collect(returned), slot_safe, axis=0) * row_live
    block_out = x_one + gate_vals * expert_rows * row_live
    grad_out = cotangent.astype(jnp.float32)
    grad_gate = jnp.sum(grad_out * expert_rows, axis=1, keepdims=True) * row_live
    grad_expert = (gate_vals * row_live * grad_out).astype(jnp.bfloat16)
    send_grads = spread(matmul(dispatch, grad_expert).astype(jnp.bfloat16))
    rows_again, grads_in = (
        lax.all_to_all(send_rows, "dp", split_axis=0, concat_axis=0, tiled=True),
        lax.all_to_all(send_grads, "dp", split_axis=0, concat_axis=0, tiled=True),
    )
    rows_back = rows_again.reshape(-1, model_width)
    pre_back = matmul(rows_back, w_in)
    act_back, gelu_pull = jax.vjp(lambda inner: jax.nn.gelu(inner, approximate=True), pre_back)
    act_low = act_back.astype(jnp.bfloat16)
    grad_rows = grads_in.reshape(-1, model_width)
    grad_act = jnp.einsum("sd,fd->sf", grad_rows, w_out, preferred_element_type=jnp.float32)
    grad_w_out = jnp.einsum("sf,sd->fd", act_low, grad_rows, preferred_element_type=jnp.float32)
    grad_pre = gelu_pull(grad_act)[0].astype(jnp.bfloat16)
    grad_w_in = jnp.einsum("sd,sf->df", rows_back, grad_pre, preferred_element_type=jnp.float32)
    grad_sent = jnp.einsum("sf,df->sd", grad_pre, w_in, preferred_element_type=jnp.float32).astype(
        jnp.bfloat16
    )
    grad_back = lax.all_to_all(
        grad_sent.reshape(-1, capacity, model_width), "dp", split_axis=0, concat_axis=0, tiled=True
    )
    grad_h_two = jnp.take(collect(grad_back), slot_safe, axis=0) * row_live
    grad_probs = route_onehot.astype(jnp.float32) * grad_gate
    grad_logits = router_probs * (
        grad_probs - jnp.sum(router_probs * grad_probs, axis=1, keepdims=True)
    )
    grad_router = jnp.dot(h_two.astype(jnp.float32).T, grad_logits, precision=HIGH)
    grad_h_two = grad_h_two + jnp.dot(
        grad_logits, router_full.astype(jnp.float32).T, precision=HIGH
    )
    _, norm_two_pull = jax.vjp(rms_scale, x_one, gain_second)
    grad_x_norm, grad_gain_two = norm_two_pull(grad_h_two)
    grad_x_one = grad_out + grad_x_norm
    grad_branch = (grad_x_one * row_live).astype(jnp.bfloat16)
    grad_w_output = jnp.einsum(
        "td,te->de", mixture, grad_branch, preferred_element_type=jnp.float32
    )
    grad_mix = jnp.einsum("te,de->td", grad_branch, output_full, preferred_element_type=jnp.float32)
    grad_mix_heads = grad_mix.astype(jnp.bfloat16).reshape(row_count, HEADS, HEAD)
    terms_again, bias_pull = jax.vjp(
        lambda grid_in: bias_block(grid_in, bucket_ids, first_row, row_count, group_rows),
        table_float,
    )
    scores_again = masked_scores(q_heads, k_heads, terms_again, allowed)
    probs_again = jnp.exp(scores_again - log_total)
    grad_probs_att = jnp.einsum(
        "qhd,khd->hqk", grad_mix_heads, v_heads, preferred_element_type=jnp.float32
    )
    row_dot = jnp.sum(probs_again * grad_probs_att, axis=-1, keepdims=True)
    grad_scores = probs_again * (grad_probs_att - row_dot)
    grad_table = bias_pull(grad_scores)[0]
    grad_scores_low = grad_scores.astype(jnp.bfloat16)
    score_scale = HEAD ** (-0.5)
    grad_q = (
        jnp.einsum("hqk,khd->qhd", grad_scores_low, k_heads, preferred_element_type=jnp.float32)
        * score_scale
    )
    grad_q = grad_q.reshape(row_count, model_width).astype(jnp.bfloat16)
    grad_k_part = (
        jnp.einsum("hqk,qhd->khd", grad_scores_low, q_heads, preferred_element_type=jnp.float32)
        * score_scale
    )
    grad_v_part = jnp.einsum(
        "hqk,qhd->khd",
        probs_again.astype(jnp.bfloat16),
        grad_mix_heads,
        preferred_element_type=jnp.float32,
    )
    grad_k_sum, grad_v_sum = (
        lax.psum_scatter(
            grad_k_part.reshape(group_rows, model_width).astype(jnp.bfloat16),
            "rep",
            scatter_dimension=0,
            tiled=True,
        ).astype(jnp.float32),
        lax.psum_scatter(
            grad_v_part.reshape(group_rows, model_width).astype(jnp.bfloat16),
            "rep",
            scatter_dimension=0,
            tiled=True,
        ).astype(jnp.float32),
    )
    grad_k = grad_k_sum.astype(jnp.bfloat16)
    grad_v = grad_v_sum.astype(jnp.bfloat16)
    grad_w_query = jnp.einsum("td,te->de", h_one, grad_q, preferred_element_type=jnp.float32)
    grad_w_key = jnp.einsum("td,te->de", h_one, grad_k, preferred_element_type=jnp.float32)
    grad_w_value = jnp.einsum("td,te->de", h_one, grad_v, preferred_element_type=jnp.float32)
    grad_h_one = jnp.einsum("te,de->td", grad_q, query_full, preferred_element_type=jnp.float32)
    grad_h_one = grad_h_one + jnp.einsum(
        "te,de->td", grad_k, key_full, preferred_element_type=jnp.float32
    )
    grad_h_one = grad_h_one + jnp.einsum(
        "te,de->td", grad_v, value_full, preferred_element_type=jnp.float32
    )
    _, norm_one_pull = jax.vjp(rms_scale, x_in, gain_first)
    grad_x_in, grad_gain_one = norm_one_pull(grad_h_one)
    grad_input = grad_x_one + grad_x_in
    shares = (
        lax.psum_scatter(grad_gain_one, "dp", scatter_dimension=0, tiled=True),
        lax.psum_scatter(grad_w_query, "dp", scatter_dimension=0, tiled=True),
        lax.psum_scatter(grad_w_key, "dp", scatter_dimension=0, tiled=True),
        lax.psum_scatter(grad_w_value, "dp", scatter_dimension=0, tiled=True),
        lax.psum_scatter(grad_w_output, "dp", scatter_dimension=0, tiled=True),
        lax.psum_scatter(grad_table, "dp", scatter_dimension=0, tiled=True),
        lax.psum_scatter(grad_gain_two, "dp", scatter_dimension=0, tiled=True),
        lax.psum_scatter(grad_router, "dp", scatter_dimension=0, tiled=True),
    )
    (
        share_gain_one,
        share_query,
        share_key,
        share_value,
        share_output,
        share_table,
        share_gain_two,
        share_router,
    ) = shares
    small_sums = lax.psum((share_gain_one, share_table, share_gain_two, share_router), "rep")
    pieces = (
        lax.psum_scatter(
            share_query.astype(jnp.bfloat16), "rep", scatter_dimension=1, tiled=True
        ).astype(jnp.float32),
        lax.psum_scatter(
            share_key.astype(jnp.bfloat16), "rep", scatter_dimension=1, tiled=True
        ).astype(jnp.float32),
        lax.psum_scatter(
            share_value.astype(jnp.bfloat16), "rep", scatter_dimension=1, tiled=True
        ).astype(jnp.float32),
        lax.psum_scatter(
            share_output.astype(jnp.bfloat16), "rep", scatter_dimension=1, tiled=True
        ).astype(jnp.float32),
        lax.psum_scatter(
            grad_w_in.astype(jnp.bfloat16), "rep", scatter_dimension=1, tiled=True
        ).astype(jnp.float32),
        lax.psum_scatter(
            grad_w_out.astype(jnp.bfloat16), "rep", scatter_dimension=1, tiled=True
        ).astype(jnp.float32),
    )
    full_sums = (
        lax.all_gather(pieces[0].astype(jnp.bfloat16), "rep", axis=1, tiled=True).astype(
            jnp.float32
        ),
        lax.all_gather(pieces[1].astype(jnp.bfloat16), "rep", axis=1, tiled=True).astype(
            jnp.float32
        ),
        lax.all_gather(pieces[2].astype(jnp.bfloat16), "rep", axis=1, tiled=True).astype(
            jnp.float32
        ),
        lax.all_gather(pieces[3].astype(jnp.bfloat16), "rep", axis=1, tiled=True).astype(
            jnp.float32
        ),
        lax.all_gather(pieces[4].astype(jnp.bfloat16), "rep", axis=1, tiled=True).astype(
            jnp.float32
        ),
        lax.all_gather(pieces[5].astype(jnp.bfloat16), "rep", axis=1, tiled=True).astype(
            jnp.float32
        ),
    )
    return (
        block_out.astype(jnp.bfloat16),
        grad_input,
        small_sums[0],
        full_sums[0],
        full_sums[1],
        full_sums[2],
        full_sums[3],
        small_sums[1],
        small_sums[2],
        small_sums[3],
        full_sums[4],
        full_sums[5],
    )


def solution(mesh):
    placed = (
        P(("dp", "rep"), None),
        P("dp", None),
        P(),
        P(("dp", "rep"), None),
        P("dp"),
        P("dp", None),
        P("dp", None),
        P("dp", None),
        P("dp", None),
        P("dp"),
        P("dp"),
        P("dp", None),
        P(None, "dp"),
        P("dp", None),
        P(("dp", "rep"), None),
    )
    return jax.shard_map(
        on_device,
        mesh=mesh,
        in_specs=placed,
        out_specs=(
            P(("dp", "rep"), None),
            P(("dp", "rep"), None),
            P("dp"),
            P("dp", None),
            P("dp", None),
            P("dp", None),
            P("dp", None),
            P("dp"),
            P("dp"),
            P("dp", None),
            P(None, "dp"),
            P("dp", None),
        ),
        check_vma=False,
    )
```

profile of v0, /device:TPU:13, one launch (start us, length us, event | category | flops | bytes accessed | tf_op | source)
XLA Modules:
  0.0 1408.4 jit_solution(11628442604875571847)
XLA Ops:
  15.2 12.4 all-reduce.8
  30.0 217.1 %gather_fusion = f32[65536,12]{1,0:T(8,128)} fusion(f32[12,1023]{0,1:T(8,128)S(1)} %fusion.30, s32[65536]{0:T(1024)S(1)} %broadcast_clamp_fusion), kind=kCustom, calls=%fused_computation.2 | custom fusion | bytes 6553600 | tf_op jit(solution)/shard_map/gather | solution.py:35
  247.1 20.8 %copy.91 = f32[128,512,12]{1,0,2:T(8,128)} copy(f32[128,512,12]{2,1,0:T(8,128)} %bitcast.94) | data formatting | bytes 6291456 | tf_op jit(solution)/shard_map/gather | solution.py:35
  273.3 12.2 all_gather.50
  290.2 8.7 all_gather.53
  300.1 2.9 fusion.70
  310.3 10.5 all-to-all-start
  321.9 6.7 all-to-all-done
  330.4 3.3 fusion.72
  334.9 4.2 convolution_convert_fusion.4
  340.8 5.8 all-to-all-start.1
  347.9 19.6 %all-gather = bf16[8,96,8]{1,2,0:T(8,128)(2,1)S(1)} all-gather(bf16[1,96,8]{1,2,0:T(8,128)(2,1)S(1)} %bitcast.125), channel_id=1, replica_groups=mesh['dp'=8,'rep'=4] {'dp'}, dimensions={0}, use_global_device_ids=true | all-gather | bytes 13824 | tf_op jit(solution)/shard_map/all_gather | solution.py:75
  373.3 2.8 gather_fusion.1
  384.6 13.1 all_to_all.21
  399.4 5.0 fusion.8
  405.3 4.7 convolution_convert_fusion.3
  411.7 11.7 all_to_all.22
  425.2 2.9 gather_fusion.2
  428.0 2.4 multiply_reduce_fusion.1
  431.1 2.1 convert_add_fusion
  436.9 2.3 multiply_reduce_fusion
  443.7 2.3 copy.93
  446.0 2.6 convolution_convert_fusion.2
  448.6 2.4 copy.95
  451.8 2.1 fusion.63
  457.0 18.6 %reduce-scatter.40.cloned.1.call-done = bf16[128,768]{1,0:T(8,128)(2,1)} async-done(((bf16[512,768]{1,0:T(8,128)(2,1)}), bf16[128,768]{1,0:T(8,128)(2,1)}) %reduce-scatter.40.cloned.1.call-update) | async-done | bytes 196624
  475.6 2.9 fusion.61
  478.5 22.9 %reduce-scatter.42.cloned.1.call-done = bf16[128,768]{1,0:T(8,128)(2,1)} async-done(((bf16[512,768]{1,0:T(8,128)(2,1)}), bf16[128,768]{1,0:T(8,128)(2,1)}) %reduce-scatter.42.cloned.1.call-update) | async-done | bytes 196624
  501.4 2.9 fusion.59
  505.6 3.6 convolution_convert_fusion.1
  510.7 3.7 convolution_convert_fusion
  516.3 55.0 %reduce-scatter.28.cloned.1.call-done = f32[96,768]{1,0:T(8,128)} async-done(((f32[768,768]{1,0:T(8,128)}), f32[96,768]{1,0:T(8,128)}) %reduce-scatter.28.cloned.1.call-update) | async-done | bytes 294928 | tf_op jit(solution)/shard_map/reduce_scatter | solution.py:249
  573.1 69.7 %reduce-scatter.34.cloned.1.call-done = f32[96,768]{1,0:T(8,128)} async-done(((f32[768,768]{1,0:T(8,128)}), f32[96,768]{1,0:T(8,128)}) %reduce-scatter.34.cloned.1.call-update) | async-done | bytes 294928 | tf_op jit(solution)/shard_map/reduce_scatter | solution.py:252
  644.7 69.7 %reduce-scatter.30.cloned.1.call-done = f32[96,768]{1,0:T(8,128)} async-done(((f32[768,768]{1,0:T(8,128)}), f32[96,768]{1,0:T(8,128)}) %reduce-scatter.30.cloned.1.call-update) | async-done | bytes 294928 | tf_op jit(solution)/shard_map/reduce_scatter | solution.py:250
  716.3 69.7 %reduce-scatter.32.cloned.1.call-done = f32[96,768]{1,0:T(8,128)} async-done(((f32[768,768]{1,0:T(8,128)}), f32[96,768]{1,0:T(8,128)}) %reduce-scatter.32.cloned.1.call-update) | async-done | bytes 294928 | tf_op jit(solution)/shard_map/reduce_scatter | solution.py:251
  788.0 50.8 %reduce-scatter.36.cloned.1.call-done = bf16[768,768]{1,0:T(8,128)(2,1)} async-done(((bf16[768,3072]{1,0:T(8,128)(2,1)}), bf16[768,768]{1,0:T(8,128)(2,1)}) %reduce-scatter.36.cloned.1.call-update) | async-done | bytes 1179664 | tf_op jit(solution)/shard_map/reduce_scatter | solution.py:281
  838.8 51.0 %reduce-scatter.38.cloned.1.call-done = bf16[3072,192]{0,1:T(8,128)(2,1)} async-done(((bf16[3072,768]{0,1:T(8,128)(2,1)}), bf16[3072,192]{0,1:T(8,128)(2,1)}) %reduce-scatter.38.cloned.1.call-update) | async-done | bytes 1179664 | tf_op jit(solution)/shard_map/reduce_scatter | solution.py:284
  891.1 61.0 %reduce-scatter.52.cloned.1.call-done = f32[96,8]{1,0:T(8,128)} async-done(((f32[768,8]{1,0:T(8,128)}), f32[96,8]{1,0:T(8,128)}) %reduce-scatter.52.cloned.1.call-update) | async-done | bytes 3088
  953.0 16.8 %copy.92 = f32[128,512,12]{2,1,0:T(8,128)} copy(f32[128,512,12]{1,0,2:T(8,128)S(1)} %copy-done.3) | data formatting | bytes 6291456 | tf_op jit(solution)/shard_map/mul | solution.py:199
  969.8 347.6 %scatter_custom_fusion = f32[12,1023]{0,1:T(8,128)S(1)} fusion(s32[65536]{0:T(1024)} %bitcast.111, f32[65536,12]{1,0:T(8,128)} %bitcast.95, f32[]{:T(128)} %constant.32.clone.1), kind=kCustom, calls=%fused_computation.71 | custom fusion | flops 786432 | bytes 49616 | tf_op jit(solution)/shard_map/transpose(jvp())/scatter-add | solution.py:35
  1321.2 22.3 %all-reduce.6 = (f32[768]{0:T(1024)S(1)}, f32[384]{0:T(512)S(1)}, f32[768]{0:T(1024)S(1)}) all-reduce(f32[768]{0:T(1024)S(1)} %get-tuple-element.63, f32[384]{0:T(512)S(1)} %reshape.272, f32[768]{0:T(1024)S(1)} %copy-done.37), channel_id=4, replica_groups=mesh['dp'=8,'rep'=4] {'dp'}, use_global_device_ids=true, to_apply=%region_19.21.clone | all-reduce | flops 1920 | bytes 15360
  1343.7 15.3 %all-reduce.7 = (f32[96]{0:T(128)}, f32[48]{0:T(128)}, f32[96]{0:T(128)}, f32[96,8]{0,1:T(8,128)}) all-reduce(f32[96]{0:T(128)S(1)} %dynamic-slice.4, f32[48]{0:T(128)S(1)} %dynamic-slice.6, f32[96]{0:T(128)S(1)} %dynamic-slice.8, f32[96,8]{0,1:T(8,128)S(1)} %copy.106), channel_id=1, replica_groups=mesh['dp'=8,'rep'=4] {'rep'}, use_global_device_ids=true, to_apply=%region_20.22 | all-reduce | flops 1008 | bytes 8064 | tf_op jit(solution)/shard_map/psum | solution.py:267
  1359.9 6.3 all_gather.58
  1367.1 5.8 all_gather.61
  1373.8 5.8 all_gather.59
  1380.4 5.8 all_gather.60
  1387.1 7.4 convert_element_type.223
  1394.5 7.4 copy.89
  (247 shorter events, 88.7 us)
Async XLA Ops:
  7.2 22.5 %copy-start.35 = (s32[1023]{0:T(1024)S(1)}, s32[1023]{0:T(1024)}, u32[]{:S(2)}) copy-start(s32[1023]{0:T(1024)} %param.19) | copy-start | bytes 12280
  7.2 264.5 %all-gather.8.cloned.1.call-start = ((), (), s32[]{:S(2)}) async-start(), calls=%async_computation.17 | async-start | bytes 1327104 | tf_op jit(solution)/shard_map/all_gather | solution.py:71
  7.9 278.8 %all-gather.10.cloned.1.call-start = ((), (), s32[]{:S(2)}) async-start(), calls=%async_computation.18 | async-start | bytes 1327104 | tf_op jit(solution)/shard_map/all_gather | solution.py:69
  8.7 279.9 %all-gather.12.cloned.1.call-start = ((), (), s32[]{:S(2)}) async-start(), calls=%async_computation.19 | async-start | bytes 1327104 | tf_op jit(solution)/shard_map/all_gather | solution.py:70
  9.4 295.6 %all-gather.14.cloned.1.call-start = ((), (), s32[]{:S(2)}) async-start(), calls=%async_computation.20 | async-start | bytes 1327104 | tf_op jit(solution)/shard_map/all_gather | solution.py:72
  28.6 218.5 %copy-start.49 = (f32[128]{0:T(128)}, f32[128]{0:T(128)S(1)}, u32[]{:S(2)}) copy-start(f32[128]{0:T(128)S(1)} %fusion.22) | copy-start | bytes 1540
  28.7 259.9 %copy-start.29 = (f32[128]{0:T(128)}, f32[128]{0:T(128)S(1)}, u32[]{:S(2)}) copy-start(f32[128]{0:T(128)S(1)} %fusion.52) | copy-start | bytes 1540
  247.1 20.8 %copy-start.52 = (s32[1,3]{1,0:T(1,128)S(1)}, s32[1,3]{1,0:T(1,128)}, u32[]{:S(2)}) copy-start(s32[1,3]{1,0:T(1,128)} %param.18) | copy-start | bytes 40
  247.1 23.6 %copy-start.33 = (s32[128,1]{0,1:T(1,128)S(1)}, s32[128,1]{0,1:T(1,128)}, u32[]{:S(2)}) copy-start(s32[128,1]{0,1:T(1,128)} %param.20) | copy-start | bytes 1540
  247.1 24.6 %copy-start = (bf16[128,768]{1,0:T(8,128)(2,1)S(1)}, bf16[128,768]{1,0:T(8,128)(2,1)}, u32[]{:S(2)}) copy-start(bf16[128,768]{1,0:T(8,128)(2,1)} %param.17) | copy-start | bytes 589828
  270.8 15.9 %copy-start.40 = (pred[128]{0:T(512)(128)(4,1)}, pred[128]{0:T(512)(128)(4,1)S(1)}, u32[]{:S(2)}) copy-start(pred[128]{0:T(512)(128)(4,1)S(1)} %get-tuple-element.80) | copy-start | bytes 388
  270.8 36.1 %copy-start.28 = (f32[768]{0:T(1024)}, f32[768]{0:T(1024)S(1)}, u32[]{:S(2)}) copy-start(f32[768]{0:T(1024)S(1)} %convert_element_type.190) | copy-start | bytes 9220
  288.5 11.6 copy-start.22
  305.0 1.9 copy-start.16
  305.0 2.7 copy-start.42
  310.3 18.3 %all-to-all-start = ((bf16[8,18,768]{2,1,0:T(8,128)(2,1)}), bf16[8,18,768]{2,1,0:T(8,128)(2,1)}, u32[]{:S(2)}, u32[]{:S(2)}) async-start(bf16[8,18,768]{2,1,0:T(8,128)(2,1)} %reshape_reshape.6), calls=%async_computation | async-start | bytes 589824 | tf_op jit(solution)/shard_map/all_to_all | solution.py:137
  334.9 13.0 copy-start.48
  340.8 30.7 %all-to-all-start.1 = ((bf16[8,18,768]{2,1,0:T(8,128)(2,1)}), bf16[8,18,768]{2,1,0:T(8,128)(2,1)}, u32[]{:S(2)}, u32[]{:S(2)}) async-start(bf16[8,18,768]{2,1,0:T(8,128)(2,1)} %reshape.264), calls=%async_computation.1 | async-start | bytes 589824 | tf_op jit(solution)/shard_map/all_to_all | solution.py:145
  346.6 129.0 %reduce-scatter.40.cloned.1.call-start = ((), (), s32[]{:S(2)}) async-start(), calls=%async_computation.29 | async-start | bytes 983040
  428.0 5.9 copy-start.12
  428.0 5.9 copy-start.31
  439.2 3.2 copy-start.23
  446.0 55.4 %reduce-scatter.42.cloned.1.call-start = ((), (), s32[]{:S(2)}) async-start(), calls=%async_computation.30 | async-start | bytes 983040
  448.6 2.5 copy-start.2
  448.6 2.5 copy-start.5
  451.1 120.2 %reduce-scatter.28.cloned.1.call-start = ((), (), s32[]{:S(2)}) async-start(), calls=%async_computation.21 | async-start | bytes 2654208 | tf_op jit(solution)/shard_map/reduce_scatter | solution.py:249
  451.8 2.1 copy-start.18
  453.9 188.9 %reduce-scatter.34.cloned.1.call-start = ((), (), s32[]{:S(2)}) async-start(), calls=%async_computation.24 | async-start | bytes 2654208 | tf_op jit(solution)/shard_map/reduce_scatter | solution.py:252
  456.9 257.5 %reduce-scatter.30.cloned.1.call-start = ((), (), s32[]{:S(2)}) async-start(), calls=%async_computation.22 | async-start | bytes 2654208 | tf_op jit(solution)/shard_map/reduce_scatter | solution.py:250
  478.5 307.6 %reduce-scatter.32.cloned.1.call-start = ((), (), s32[]{:S(2)}) async-start(), calls=%async_computation.23 | async-start | bytes 2654208 | tf_op jit(solution)/shard_map/reduce_scatter | solution.py:251
  504.4 334.4 %reduce-scatter.36.cloned.1.call-start = ((), (), s32[]{:S(2)}) async-start(), calls=%async_computation.25 | async-start | bytes 5898240 | tf_op jit(solution)/shard_map/reduce_scatter | solution.py:281
  509.2 380.6 %reduce-scatter.38.cloned.1.call-start = ((), (), s32[]{:S(2)}) async-start(), calls=%async_computation.27 | async-start | bytes 5898240 | tf_op jit(solution)/shard_map/reduce_scatter | solution.py:284
  514.4 437.7 %reduce-scatter.52.cloned.1.call-start = ((), (), s32[]{:S(2)}) async-start(), calls=%async_computation.35 | async-start | bytes 442368
  516.2 843.7 %reduce-scatter.44.cloned.1.call-start = ((), (), s32[]{:S(2)}) async-start(), calls=%async_computation.31 | async-start | bytes 245760
  573.1 794.0 %reduce-scatter.50.cloned.1.call-start = ((), (), s32[]{:S(2)}) async-start(), calls=%async_computation.34 | async-start | bytes 245760
  644.7 729.1 %reduce-scatter.46.cloned.1.call-start = ((), (), s32[]{:S(2)}) async-start(), calls=%async_computation.32 | async-start | bytes 245760
  716.3 236.7 %copy-start.3 = (f32[128,512,12]{1,0,2:T(8,128)S(1)}, f32[128,512,12]{1,0,2:T(8,128)}, u32[]{:S(2)}) copy-start(f32[128,512,12]{1,0,2:T(8,128)} %get-tuple-element.81) | copy-start | bytes 9437188
  716.3 664.1 %reduce-scatter.48.cloned.1.call-start = ((), (), s32[]{:S(2)}) async-start(), calls=%async_computation.33 | async-start | bytes 245760
  787.9 599.2 %all-gather.16.cloned.1.call-start = ((), (), s32[]{:S(2)}) async-start(), calls=%async_computation.26 | async-start | bytes 5898240 | tf_op jit(solution)/shard_map/all_gather | solution.py:301
  838.8 555.7 %all-gather.18.cloned.1.call-start = ((), (), s32[]{:S(2)}) async-start(), calls=%async_computation.28 | async-start | bytes 5898240 | tf_op jit(solution)/shard_map/all_gather | solution.py:304
  953.0 364.4 %copy-start.36 = (s32[1023]{0:T(1024)S(1)}, s32[1023]{0:T(1024)}, u32[]{:S(2)}) copy-start(s32[1023]{0:T(1024)} %param.19) | copy-start | bytes 12280
  953.0 365.0 %copy-start.19 = (bf16[12,64,128]{2,1,0:T(8,128)(2,1)S(1)}, bf16[12,64,128]{2,1,0:T(8,128)(2,1)}, u32[]{:S(2)}) copy-start(bf16[12,64,128]{2,1,0:T(8,128)(2,1)} %copy-done.18) | copy-start | bytes 589828
  969.8 350.2 %copy-start.11 = (bf16[768,768]{1,0:T(8,128)(2,1)S(1)}, bf16[768,768]{1,0:T(8,128)(2,1)}, u32[]{:S(2)}) copy-start(bf16[768,768]{1,0:T(8,128)(2,1)} %all-gather.12.cloned.1.call-done) | copy-start | bytes 3538948
  1318.0 2.0 copy-start.25
  1318.0 2.5 copy-start.10
  1318.0 2.5 copy-start.26
  1320.0 39.0 %copy-start.50 = (f32[128]{0:T(128)S(1)}, f32[128]{0:T(128)}, u32[]{:S(2)}) copy-start(f32[128]{0:T(128)} %copy-done.49) | copy-start | bytes 1540
  1320.0 39.0 %copy-start.9 = (f32[128,768]{1,0:T(8,128)S(1)}, f32[128,768]{1,0:T(8,128)}, u32[]{:S(2)}) copy-start(f32[128,768]{1,0:T(8,128)} %copy-done.7) | copy-start | bytes 1179652
  (26 other events, 23.8 us)
Sparse Core Ops, SparseCore 0:
  10.2 39.8 all-gather.7
  52.3 39.8 all-gather.9
  94.3 39.8 all-gather.11
  136.2 39.8 all-gather.13
  446.1 29.4 reduce-scatter.39
  478.1 23.2 reduce-scatter.41
  504.9 66.2 reduce-scatter.27
  574.7 68.0 reduce-scatter.33
  646.3 68.0 reduce-scatter.29
  717.8 68.2 reduce-scatter.31
  789.2 49.5 reduce-scatter.35
  841.9 47.8 reduce-scatter.37
  893.1 59.0 reduce-scatter.51
  955.0 20.9 reduce-scatter.43
  978.3 19.7 reduce-scatter.49
  1000.4 19.7 reduce-scatter.45
  1022.5 19.7 reduce-scatter.47
  1043.7 38.0 all-gather.15
  1083.3 37.4 all-gather.17
where the time goes:
time: 1420 us; the launch traced here: 1410 us
  waiting for transfers between devices  478 us (34%)
  other arithmetic  376 us (26%)
  local copies, waits for them, and re-layouts  317 us (22%)
  blocking collectives  139 us (10%)
  matrix products  64 us (5%)
  starting transfers between devices  17.2 us (1%)
  between operations  17.2 us (1%)
    scatter-add x1, other arithmetic, bias_block(): return by_offset[:, offsets]  348 us
    gather x2, local copies, waits for them, and re-layouts, bias_block(): return by_offset[:, offsets]  238 us
    unnamed x26, waiting for transfers between devices  105 us
    reduce_scatter x1, waiting for transfers between devices, on_device(): lax.psum_scatter(grad_w_value, 'dp', scatter_dimension=0, tiled=True)  69.7 us
    reduce_scatter x1, waiting for transfers between devices, on_device(): lax.psum_scatter(grad_w_key, 'dp', scatter_dimension=0, tiled=True)  69.7 us
    reduce_scatter x1, waiting for transfers between devices, on_device(): lax.psum_scatter(grad_w_output, 'dp', scatter_dimension=0, tiled=True)  69.7 us
    reduce_scatter x1, waiting for transfers between devices, on_device(): lax.psum_scatter(grad_w_query, 'dp', scatter_dimension=0, tiled=True)  55 us
    reduce_scatter x1, waiting for transfers between devices, on_device(): lax.psum_scatter(grad_w_out.astype(jnp.bfloat16), 'rep', scatter_dimensio...  51 us
  transfers between devices with their start and end apart: 21, of which 10 were waited for; matrix products, arithmetic and copies ran while one was open for 48% of the time, Pallas kernels for 0%

commit v1 on v0

v1 whole, which is shorter than its diff:
```python
import functools

import jax
import jax.numpy as jnp
from jax import lax
from jax.experimental import pallas as pl
from jax.experimental.pallas import tpu as pltpu
from jax.sharding import PartitionSpec as P

HEADS = 12
HEAD = 64
BUCKETS = 32
EXPERTS = 8


EPS = 1e-06
NEG = -1e30
HIGH = lax.Precision.HIGHEST
MESH = pl.DeviceIdType.MESH
VMEM_LIMIT = 48 * 1024 * 1024


def rms_scale(rows_in, gain_vec):
    return rows_in * lax.rsqrt(jnp.mean(rows_in * rows_in, axis=-1, keepdims=True) + EPS) * gain_vec


def matmul(left_op, right_op):
    return jnp.dot(left_op, right_op, preferred_element_type=jnp.float32)


def dot_over(left_op, right_op, left_dim, right_dim):
    return lax.dot_general(
        left_op, right_op, (((left_dim,), (right_dim,)), ((), ())), preferred_element_type=jnp.float32
    )


def exchange_kernel(jobs, sizes, in_count, *refs):
    ins, outs = refs[:in_count], refs[in_count : in_count + len(jobs)]
    sems = refs[in_count + len(jobs) :]
    axes = []
    for axis, _, _ in jobs:
        if axis not in axes:
            axes.append(axis)
    barrier = pltpu.get_barrier_semaphore()
    total = 0
    for axis in axes:
        me, count = lax.axis_index(axis), sizes[axis]
        for step in range(1, count):
            peer = lax.rem(me + step, count)
            pl.semaphore_signal(barrier, inc=1, device_id={axis: peer}, device_id_type=MESH)
        total += count - 1

    def local_and_remote(at, with_remote):
        axis, kind, source = jobs[at]
        me, count = lax.axis_index(axis), sizes[axis]
        from_ref = outs[source[1]] if isinstance(source, tuple) else ins[source]
        into_ref = outs[at]
        send, recv, own = sems[3 * at : 3 * at + 3]

        def part(peer):
            if kind == "gather":
                return from_ref
            if kind == "swap":
                return from_ref.at[peer]
            run = from_ref.shape[0] // count
            return from_ref.at[pl.ds(peer * run, run)]

        if not with_remote:
            return [pltpu.make_async_copy(part(me), into_ref.at[me], own)]
        found = []
        for step in range(1, count):
            peer = lax.rem(me + step, count)
            found.append(
                pltpu.make_async_remote_copy(
                    src_ref=part(peer),
                    dst_ref=into_ref.at[me],
                    send_sem=send.at[step - 1],
                    recv_sem=recv.at[step - 1],
                    device_id={axis: peer},
                    device_id_type=MESH,
                )
            )
        return found

    first = [at for at in range(len(jobs)) if not isinstance(jobs[at][2], tuple)]
    later = [at for at in range(len(jobs)) if isinstance(jobs[at][2], tuple)]
    flying = {at: local_and_remote(at, False) for at in first}
    for at in first:
        for copy in flying[at]:
            copy.start()
    pl.semaphore_wait(barrier, total)
    first.sort(key=lambda at: not any(jobs[other][2] == ("out", at) for other in later))
    for at in first:
        more = local_and_remote(at, True)
        for copy in more:
            copy.start()
        flying[at] += more
    for at in later:
        for copy in flying.pop(jobs[at][2][1]):
            copy.wait()
        flying[at] = local_and_remote(at, False) + local_and_remote(at, True)
        for copy in flying[at]:
            copy.start()
    for copies in flying.values():
        for copy in copies:
            copy.wait()


def exchange(mark, jobs, *arrays):
    sizes = {"dp": lax.axis_size("dp"), "rep": lax.axis_size("rep")}
    shapes = []
    for axis, kind, source in jobs:
        like = shapes[source[1]] if isinstance(source, tuple) else arrays[source]
        count = sizes[axis]
        if kind == "gather":
            shape = (count,) + tuple(like.shape)
        elif kind == "swap":
            shape = tuple(like.shape)
        else:
            shape = (count, like.shape[0] // count) + tuple(like.shape[1:])
        shapes.append(jax.ShapeDtypeStruct(shape, like.dtype))
    scratch = []
    for axis, _, _ in jobs:
        scratch += [
            pltpu.SemaphoreType.DMA((sizes[axis] - 1,)),
            pltpu.SemaphoreType.DMA((sizes[axis] - 1,)),
            pltpu.SemaphoreType.DMA,
        ]
    return pl.pallas_call(
        functools.partial(exchange_kernel, jobs, sizes, len(arrays)),
        out_shape=tuple(shapes),
        in_specs=[pl.BlockSpec(memory_space=pl.ANY)] * len(arrays),
        out_specs=tuple([pl.BlockSpec(memory_space=pl.ANY)] * len(jobs)),
        scratch_shapes=scratch,
        compiler_params=pltpu.CompilerParams(collective_id=mark, has_side_effects=True),
        name="exchange_%d" % mark,
    )(*arrays)


def attend_kernel(heads, block, qkv_ref, line_ref, seg_col_ref, seg_row_ref, probs_ref, mix_ref):
    rows = qkv_ref.shape[0]
    width = heads * HEAD
    for head in range(heads):
        low = head * HEAD
        k_head = qkv_ref[:, width + low : width + low + HEAD]
        v_head = qkv_ref[:, 2 * width + low : 2 * width + low + HEAD]
        line = line_ref[head : head + 1, :]
        span = line.shape[1]
        for start in range(0, rows, block):
            q_part = qkv_ref[start : start + block, low : low + HEAD]
            bias = pltpu.roll(
                jnp.broadcast_to(line, (block, span)), start, 1, stride=1, stride_axis=0
            )[:, :rows]
            scores = dot_over(q_part, k_head, 1, 1) * HEAD ** (-0.5) + bias
            allowed = seg_col_ref[start : start + block, :] == seg_row_ref[...]
            scores = jnp.where(allowed, scores, NEG)
            raised = jnp.exp(scores - jnp.max(scores, axis=-1, keepdims=True))
            probs = raised * (1.0 / jnp.sum(raised, axis=-1, keepdims=True))
            probs_ref[head, start : start + block, :] = probs
            mix_ref[start : start + block, low : low + HEAD] = matmul(
                probs.astype(jnp.bfloat16), v_head
            ).astype(jnp.bfloat16)


def attend(qkv, line, seg_col, seg_row, heads, block):
    rows = qkv.shape[0]
    return pl.pallas_call(
        functools.partial(attend_kernel, heads, block),
        out_shape=(
            jax.ShapeDtypeStruct((heads, rows, rows), jnp.float32),
            jax.ShapeDtypeStruct((rows, heads * HEAD), jnp.bfloat16),
        ),
        compiler_params=pltpu.CompilerParams(vmem_limit_bytes=VMEM_LIMIT),
        name="attend",
    )(qkv, line, seg_col, seg_row)


def attend_back_kernel(heads, block, qkv_ref, dmix_ref, probs_ref, dqkv_ref, dline_ref):
    rows = qkv_ref.shape[0]
    width = heads * HEAD
    span = dline_ref.shape[1]
    scale = HEAD ** (-0.5)
    for head in range(heads):
        low = head * HEAD
        k_head = qkv_ref[:, width + low : width + low + HEAD]
        v_head = qkv_ref[:, 2 * width + low : 2 * width + low + HEAD]
        dk = jnp.zeros((rows, HEAD), jnp.float32)
        dv = jnp.zeros((rows, HEAD), jnp.float32)
        dline = jnp.zeros((1, span), jnp.float32)
        for start in range(0, rows, block):
            q_part = qkv_ref[start : start + block, low : low + HEAD]
            dmix = dmix_ref[start : start + block, low : low + HEAD]
            probs = probs_ref[head, start : start + block, :]
            dprobs = dot_over(dmix, v_head, 1, 1)
            dscores = probs * (dprobs - jnp.sum(probs * dprobs, axis=-1, keepdims=True))
            low_scores = dscores.astype(jnp.bfloat16)
            dqkv_ref[start : start + block, low : low + HEAD] = (
                matmul(low_scores, k_head) * scale
            ).astype(jnp.bfloat16)
            dk = dk + dot_over(low_scores, q_part, 0, 0)
            dv = dv + dot_over(probs.astype(jnp.bfloat16), dmix, 0, 0)
            fold = jnp.concatenate(
                [dscores, jnp.zeros((block, span - rows), jnp.float32)], axis=1
            )
            half = block // 2
            while half >= 1:
                fold = fold[:half] + pltpu.roll(fold[half:], span - half, 1)
                half //= 2
            dline = dline + (pltpu.roll(fold, span - start, 1) if start else fold)
        dqkv_ref[:, width + low : width + low + HEAD] = (dk * scale).astype(jnp.bfloat16)
        dqkv_ref[:, 2 * width + low : 2 * width + low + HEAD] = dv.astype(jnp.bfloat16)
        dline_ref[head : head + 1, :] = dline


def attend_back(qkv, dmix, probs, heads, block):
    rows = qkv.shape[0]
    return pl.pallas_call(
        functools.partial(attend_back_kernel, heads, block),
        out_shape=(
            jax.ShapeDtypeStruct(qkv.shape, jnp.bfloat16),
            jax.ShapeDtypeStruct((heads, 2 * rows), jnp.float32),
        ),
        compiler_params=pltpu.CompilerParams(vmem_limit_bytes=VMEM_LIMIT),
        name="attend_back",
    )(qkv, dmix, probs)


def packed(parts, lead):
    flat = jnp.concatenate([piece.reshape(lead + (-1,)) for piece in parts], axis=-1)
    count = flat.shape[-1]
    whole = -(-count // 1024) * 1024
    flat = jnp.pad(flat, [(0, 0)] * len(lead) + [(0, whole - count)])
    return flat.reshape(lead + (whole // 128, 128))


def unpacked(flat, widths):
    found, at = [], 0
    for width in widths:
        found.append(flat[..., at : at + width])
        at += width
    return found


def local_columns(full, width, place):
    return lax.dynamic_slice_in_dim(full, place * width, width, axis=1)


def on_device(
    tokens,
    seq_lengths,
    bucket_ids,
    routes,
    norm1_gain,
    w_query,
    w_key,
    w_value,
    w_output,
    rel_bias,
    norm2_gain,
    w_router,
    w_in,
    w_out,
    cotangent,
):
    row_count, model_width = tokens.shape
    dp_count, rep_count = lax.axis_size("dp"), lax.axis_size("rep")
    rep_at = lax.axis_index("rep")
    group_rows = row_count * rep_count
    first_row = rep_at * row_count
    split_count = dp_count // EXPERTS
    capacity = row_count // 8 + row_count // 64
    heads = HEADS // rep_count
    width = heads * HEAD
    shard = w_query.shape[0]
    low_type = jnp.bfloat16

    piece_qkv = jnp.concatenate(
        [local_columns(full, width, rep_at) for full in (w_query, w_key, w_value)], axis=1
    )
    piece_out = local_columns(w_output, width, rep_at)
    small_widths = (shard, shard, rel_bias.shape[0], shard * EXPERTS)
    small = packed(
        [x.astype(jnp.float32) for x in (norm1_gain, norm2_gain, rel_bias, w_router)], ()
    )
    qkv_parts, out_parts, small_parts, token_parts, out_rows = exchange(
        1,
        (
            ("dp", "gather", 0),
            ("dp", "gather", 1),
            ("dp", "gather", 2),
            ("rep", "gather", 3),
            ("rep", "blocks", ("out", 1)),
        ),
        piece_qkv,
        piece_out,
        small,
        tokens,
    )
    w_qkv = qkv_parts.reshape(model_width, 3 * width)
    w_out_rows = (
        out_rows.reshape(rep_count, width, width).transpose(1, 0, 2).reshape(width, model_width)
    )
    gain_one, gain_two, table_flat, router_flat = unpacked(
        small_parts.reshape(dp_count, -1), small_widths
    )
    gain_first = gain_one.reshape(model_width)
    gain_second = gain_two.reshape(model_width)
    router_full = router_flat.reshape(model_width, EXPERTS).astype(low_type)
    table = lax.dynamic_slice_in_dim(table_flat.reshape(HEADS, BUCKETS), rep_at * heads, heads, 0)

    seq_ends = jnp.cumsum(seq_lengths[0])
    places = jnp.arange(group_rows, dtype=jnp.int32)
    segment = jnp.sum((places[:, None] >= seq_ends[None, :]).astype(jnp.int32), axis=1)
    live_bool = first_row + jnp.arange(row_count, dtype=jnp.int32) < seq_ends[-1]
    row_live = live_bool.astype(jnp.float32)[:, None]
    x_in = tokens.astype(jnp.float32)
    x_group = token_parts.reshape(group_rows, model_width).astype(jnp.float32)
    h_one = rms_scale(x_group, gain_first).astype(low_type)
    qkv = matmul(h_one, w_qkv).astype(low_type)

    by_step = jnp.concatenate(
        [
            bucket_ids[group_rows - 1 :: -1],
            jnp.full((1,), -1, jnp.int32),
            bucket_ids[: group_rows - 1 : -1],
        ]
    )
    bucket_hot = (by_step[None, :] == jnp.arange(BUCKETS, dtype=jnp.int32)[:, None]).astype(
        jnp.float32
    )
    line = jnp.dot(table, bucket_hot, precision=HIGH)
    probs, mixture = attend(qkv, line, segment[:, None], segment[None, :], heads, row_count)

    branch_parts = matmul(mixture, w_out_rows).astype(low_type)
    (branch_got,) = exchange(
        2,
        (("rep", "swap", 0),),
        branch_parts.reshape(rep_count, row_count, model_width),
    )
    branch = jnp.sum(branch_got.astype(jnp.float32), axis=0)
    x_one = x_in + row_live * branch
    h_two = rms_scale(x_one, gain_second).astype(low_type)
    router_probs = jax.nn.softmax(matmul(h_two, router_full), axis=-1)
    route_ids = routes[:, 0]
    route_onehot = route_ids[:, None] == jnp.arange(EXPERTS, dtype=jnp.int32)[None, :]
    gate_vals = jnp.sum(router_probs * route_onehot.astype(jnp.float32), axis=1, keepdims=True)
    chosen = route_onehot & live_bool[:, None]
    before = (
        jnp.arange(row_count, dtype=jnp.int32)[:, None]
        >= jnp.arange(row_count, dtype=jnp.int32)[None, :]
    ).astype(low_type)
    counts = matmul(before, chosen.astype(low_type)).astype(jnp.int32)
    rank_in = jnp.sum(jnp.where(chosen, counts - 1, 0), axis=1)
    slot_ids = jnp.where(live_bool, route_ids * capacity + rank_in, -1)
    slot_of = jnp.arange(dp_count * capacity, dtype=jnp.int32)
    slot_of = (slot_of // (capacity * split_count)) * capacity + slot_of % capacity
    dispatch = (slot_of[:, None] == slot_ids[None, :]).astype(low_type)

    grad_out = cotangent.astype(jnp.float32)
    grad_expert = (gate_vals * row_live * grad_out).astype(low_type)
    sent = matmul(dispatch, jnp.concatenate([h_two, grad_expert], axis=1)).astype(low_type)
    (got,) = exchange(
        3, (("dp", "swap", 0),), sent.reshape(dp_count, capacity, 2 * model_width)
    )
    got = got.reshape(dp_count * capacity, 2 * model_width)
    rows_here, grads_here = got[:, :model_width], got[:, model_width:]

    def expert(rows, grads):
        pre = matmul(rows, w_in)
        act, pull = jax.vjp(lambda inner: jax.nn.gelu(inner, approximate=True), pre)
        dpre = pull(dot_over(grads, w_out, 1, 1))[0]
        return act.astype(low_type), dpre.astype(low_type)

    act_here, dpre_here = expert(rows_here, grads_here)
    back = jnp.concatenate(
        [matmul(act_here, w_out).astype(low_type), dot_over(dpre_here, w_in, 1, 1).astype(low_type)],
        axis=1,
    )
    (returned,) = exchange(
        4, (("dp", "swap", 0),), back.reshape(dp_count, capacity, 2 * model_width)
    )
    landed = dot_over(dispatch, returned.reshape(dp_count * capacity, 2 * model_width), 0, 0)
    expert_rows, grad_h_two = landed[:, :model_width], landed[:, model_width:]

    block_out = x_one + gate_vals * expert_rows * row_live
    grad_gate = jnp.sum(grad_out * expert_rows, axis=1, keepdims=True) * row_live
    grad_probs = route_onehot.astype(jnp.float32) * grad_gate
    grad_logits = router_probs * (
        grad_probs - jnp.sum(router_probs * grad_probs, axis=1, keepdims=True)
    )
    grad_router = jnp.dot(h_two.astype(jnp.float32).T, grad_logits, precision=HIGH)
    grad_h_two = grad_h_two + jnp.dot(
        grad_logits, router_full.astype(jnp.float32).T, precision=HIGH
    )
    _, norm_two_pull = jax.vjp(rms_scale, x_one, gain_second)
    grad_x_norm, grad_gain_two = norm_two_pull(grad_h_two)
    grad_x_one = grad_out + grad_x_norm
    grad_branch = (grad_x_one * row_live).astype(low_type)

    branch_all, got_all = exchange(
        5, (("rep", "gather", 0), ("rep", "gather", 1)), grad_branch, got
    )
    grad_branch_group = branch_all.reshape(group_rows, model_width)
    grad_w_output = dot_over(mixture, grad_branch_group, 0, 0).astype(low_type)
    dmix = dot_over(grad_branch_group, w_out_rows, 1, 1).astype(low_type)
    dqkv, dline = attend_back(qkv, dmix, probs, heads, row_count)
    grad_table = jnp.dot(dline, bucket_hot.T, precision=HIGH)
    grad_w_qkv = dot_over(h_one, dqkv, 0, 0).astype(low_type)
    grad_h_parts = dot_over(dqkv, w_qkv, 1, 1).astype(low_type)
    grad_h_got, grad_out_cols = exchange(
        6,
        (("rep", "swap", 0), ("rep", "swap", 1)),
        grad_h_parts.reshape(rep_count, row_count, model_width),
        grad_w_output.reshape(width, rep_count, width).transpose(1, 0, 2),
    )
    grad_h_one = jnp.sum(grad_h_got.astype(jnp.float32), axis=0)
    _, norm_one_pull = jax.vjp(rms_scale, x_in, gain_first)
    grad_x_in, grad_gain_one = norm_one_pull(grad_h_one)
    grad_input = grad_x_one + grad_x_in

    table_whole = lax.dynamic_update_slice_in_dim(
        jnp.zeros((HEADS, BUCKETS), jnp.float32), grad_table, rep_at * heads, 0
    )
    small_grads = packed(
        [
            x.reshape(dp_count, -1)
            for x in (grad_gain_one, grad_gain_two, table_whole, grad_router)
        ],
        (dp_count,),
    )
    weight_got, out_got, small_got = exchange(
        7,
        (("dp", "swap", 0), ("dp", "swap", 1), ("dp", "swap", 2)),
        grad_w_qkv.reshape(dp_count, shard, 3 * width),
        grad_out_cols.reshape(dp_count, shard, width),
        small_grads,
    )
    weight_sum = jnp.concatenate(
        [
            jnp.sum(weight_got.astype(jnp.float32), axis=0),
            jnp.sum(out_got.astype(jnp.float32), axis=0),
        ],
        axis=1,
    ).astype(low_type)
    weight_all, small_all = exchange(
        8,
        (("rep", "gather", 0), ("rep", "gather", 1)),
        weight_sum,
        jnp.sum(small_got, axis=0),
    )
    weights = (
        weight_all.reshape(rep_count, shard, 4, width)
        .transpose(2, 1, 0, 3)
        .reshape(4, shard, model_width)
        .astype(jnp.float32)
    )
    small_sum = jnp.sum(small_all, axis=0).reshape(-1)
    out_gain_one, out_gain_two, out_table, out_router = unpacked(small_sum, small_widths)

    got_all = got_all.reshape(-1, 2 * model_width)
    rows_all, grads_all = got_all[:, :model_width], got_all[:, model_width:]
    act_all, dpre_all = expert(rows_all, grads_all)
    grad_w_in = dot_over(rows_all, dpre_all, 0, 0)
    grad_w_out = dot_over(act_all, grads_all, 0, 0)
    return (
        block_out.astype(low_type),
        grad_input,
        out_gain_one,
        weights[0],
        weights[1],
        weights[2],
        weights[3],
        out_table,
        out_gain_two,
        out_router.reshape(shard, EXPERTS),
        grad_w_in,
        grad_w_out,
    )


def solution(mesh):
    placed = (
        P(("dp", "rep"), None),
        P("dp", None),
        P(),
        P(("dp", "rep"), None),
        P("dp"),
        P("dp", None),
        P("dp", None),
        P("dp", None),
        P("dp", None),
        P("dp"),
        P("dp"),
        P("dp", None),
        P(None, "dp"),
        P("dp", None),
        P(("dp", "rep"), None),
    )
    return jax.shard_map(
        on_device,
        mesh=mesh,
        in_specs=placed,
        out_specs=(
            P(("dp", "rep"), None),
            P(("dp", "rep"), None),
            P("dp"),
            P("dp", None),
            P("dp", None),
            P("dp", None),
            P("dp", None),
            P("dp"),
            P("dp"),
            P("dp", None),
            P(None, "dp"),
            P("dp", None),
        ),
        check_vma=False,
    )
```

time: 1420 us -> 322 us (0.23)
  waiting for transfers between devices: 478 us -> 0 us
  other arithmetic: 376 us -> 27.6 us
  local copies, waits for them, and re-layouts: 317 us -> 42.9 us
  Pallas kernels: 0 us -> 186 us
  blocking collectives: 139 us -> 0 us
  starting transfers between devices: 17.2 us -> 0 us
  between operations: 17.2 us -> 1.23 us
    reduce_scatter x6 -> x0, waiting for transfers between devices: 366 us -> none  [the longest x1 69.7 us: on_device(): lax.psum_scatter(grad_w_value, 'dp', scatter_dimension=0, tiled=True)]
    scatter-add x1 -> x0, other arithmetic: 348 us -> none  [bias_block(): return by_offset[:, offsets]]
    gather x4 -> x0, local copies, waits for them, and re-layouts: 244 us -> none  [the longest x2 238 us: bias_block(): return by_offset[:, offsets]]
    pallas_call x0 -> x10, Pallas kernels: none -> 186 us  [the longest x8 173 us: exchange(): pl.pallas_call(functools.partial(exchange_kernel, jobs, sizes, len(arrays...]
    unnamed x26 -> x0, waiting for transfers between devices: 105 us -> none
    all_gather x7 -> x0, blocking collectives: 64.3 us -> none  [the longest x1 19.6 us: on_device(): lax.all_gather(w_router, 'dp', axis=0, tiled=True)]
    unnamed x2 -> x0, blocking collectives: 34.7 us -> none
    unnamed x130 -> x80, local copies, waits for them, and re-layouts: 36.6 us -> 11.4 us
  transfers between devices with their start and end apart: 21 -> 0, of which waited for: 10 -> 0; matrix products, arithmetic and copies ran while one was open for 48% -> 0% of each run, Pallas kernels for 0% -> 0%
where the time goes in v1:
time: 322 us; the launch traced here: 319 us
  Pallas kernels  186 us (58%)
  matrix products  60.7 us (19%)
  local copies, waits for them, and re-layouts  42.9 us (13%)
  other arithmetic  27.6 us (9%)
    pallas_call x8, Pallas kernels, exchange(): pl.pallas_call(functools.partial(exchange_kernel, jobs, sizes, len(arrays...  173 us
    dot_general x8, matrix products, dot_over(): lax.dot_general(left_op, right_op, (((left_dim,), (right_dim,)), ((), ())...  39.3 us
    dot_general x8, matrix products, matmul(): return jnp.dot(left_op, right_op, preferred_element_type=jnp.float32)  16.8 us
    unnamed x80, local copies, waits for them, and re-layouts  11.4 us
    pallas_call x1, Pallas kernels, attend_back(): pl.pallas_call(functools.partial(attend_back_kernel, heads, block), out_s...  8.23 us

profile of v1, /device:TPU:13, one launch (start us, length us, event | category | flops | bytes accessed | tf_op | source)
XLA Modules:
  0.0 318.7 jit_solution(16606334939869848771)
XLA Ops:
  3.6 1.2 add_select_fusion
  8.0 1.4 fusion.94.refs_2_
  10.4 1.6 constant_dynamic-slice_fusion
  13.0 35.4 %exchange_1.1 = (bf16[8,96,576]{2,1,0:T(8,128)(2,1)}, bf16[8,96,192]{2,1,0:T(8,128)(2,1)}, f32[8,8,128]{2,1,0:T(8,128)}, bf16[4,128,768]{2,1,0:T(8,128)(2,1)}, bf16[4,2,96,192]{3,2,1,0:T(8,128)(2,1)}) custom-call(bf16[96,576]{1,0:T(8,128)(2,1)} %pad_maximum_fusion.2.refs_0_, bf16[96,192]{1,0:T(8,128)(2,1)} %get-tuple-element.106.refs_1_, ...), custom_call_target="tpu_custom_call" | custom-call | tf_op jit(solution)/shard_map/exchange_1/pallas_call | solution.py:129
  49.2 1.4 multiply_reduce_fusion
  52.2 1.3 copy.82
  54.5 2.3 fusion.22
  57.9 4.5 %attend.1 = (f32[3,512,512]{2,1,0:T(8,128)S(1)}, bf16[512,192]{1,0:T(8,128)(2,1)S(1)}) custom-call(bf16[512,576]{1,0:T(8,128)(2,1)S(1)} %convolution_convert_fusion.4.qkv_ref, f32[3,1024]{1,0:T(4,128)S(1)} %fusion.66.line_ref, s32[512,1]{1,0:T(8,128)S(1)} %copy.62.seg_col_ref, s32[1,512]{1,0:T(1,128)S(1)} %bitcast.72), custom_call_target="tpu_custom_call" | custom-call | tf_op jit(solution)/shard_map/attend/pallas_call | solution.py:167
  64.0 1.2 convolution_convert_fusion.3
  65.3 12.2 %exchange_2.1 = bf16[4,128,768]{2,1,0:T(8,128)(2,1)} custom-call(bf16[4,128,768]{2,1,0:T(8,128)(2,1)} %bitcast.77), custom_call_target="tpu_custom_call" | custom-call | tf_op jit(solution)/shard_map/exchange_2/pallas_call | solution.py:129
  77.4 1.3 convert_reduce_fusion.1
  82.9 1.7 convolution_convert_fusion
  84.7 2.0 reshape.267.refs_0_
  86.6 17.4 %exchange_3.1 = bf16[8,18,1536]{2,1,0:T(8,128)(2,1)} custom-call(bf16[8,18,1536]{2,1,0:T(8,128)(2,1)} %reshape.267.refs_0_), custom_call_target="tpu_custom_call" | custom-call | tf_op jit(solution)/shard_map/exchange_3/pallas_call | solution.py:129
  104.0 2.0 reshape.268.refs_1_
  106.0 3.3 %fusion.63 = f32[144,3072]{1,0:T(8,128)S(1)} fusion(bf16[768,3072]{1,0:T(8,128)(2,1)} %param.27, bf16[144,1536]{1,0:T(8,128)(2,1)} %reshape.268.refs_1_), kind=kOutput, calls=%fused_computation.94 | convolution fusion | flops 679477248 | bytes 6709248 | tf_op jit(solution)/shard_map/dot_general | solution.py:28
  109.3 1.2 copy-done.14
  110.5 3.5 %convolution_convert_fusion.7 = bf16[144,768]{1,0:T(8,128)(2,1)S(1)} fusion(bf16[3072,768]{1,0:T(8,128)(2,1)} %param.28, f32[144,3072]{1,0:T(8,128)S(1)} %fusion.63), kind=kOutput, calls=%fused_computation.41 | convolution fusion | flops 683569152 | bytes 6709248 | tf_op jit(solution)/shard_map/dot_general | solution.py:28
  114.1 8.6 %convolution_convert_fusion.6 = bf16[144,768]{1,0:T(8,128)(2,1)} fusion(bf16[768,3072]{1,0:T(8,128)(2,1)} %param.27, f32[144,3072]{1,0:T(8,128)} %copy-done.14, bf16[3072,768]{1,0:T(8,128)(2,1)} %param.28, bf16[144,1536]{1,0:T(8,128)(2,1)} %reshape.268.refs_1_), kind=kOutput, calls=%fused_computation.40 | convolution fusion | flops 1367912448 | bytes 11649024 | tf_op jit(solution)/shard_map/dot_general | solution.py:32
  122.7 1.8 pad_maximum_fusion
  124.5 2.0 reshape.269.refs_0_
  126.4 17.6 %exchange_4.1 = bf16[8,18,1536]{2,1,0:T(8,128)(2,1)} custom-call(bf16[8,18,1536]{2,1,0:T(8,128)(2,1)} %reshape.269.refs_0_), custom_call_target="tpu_custom_call" | custom-call | tf_op jit(solution)/shard_map/exchange_4/pallas_call | solution.py:129
  144.0 2.0 reshape.270
  146.0 1.4 fusion.67
  147.4 1.9 fusion.48
  149.4 2.3 multiply_reduce_fusion.1
  151.8 2.0 fusion.87
  153.8 1.2 reshape.279
  155.0 2.0 multiply_convert_fusion.5.refs_0_
  157.0 30.6 %exchange_5.1 = (bf16[4,128,768]{2,1,0:T(8,128)(2,1)}, bf16[4,144,1536]{2,1,0:T(8,128)(2,1)}) custom-call(bf16[128,768]{1,0:T(8,128)(2,1)} %multiply_convert_fusion.5.refs_0_, bf16[144,1536]{1,0:T(8,128)(2,1)} %reshape.268.refs_1_), custom_call_target="tpu_custom_call" | custom-call | tf_op jit(solution)/shard_map/exchange_5/pallas_call | solution.py:129
  187.7 2.3 convolution_convert_fusion.8
  190.0 2.2 convolution_convert_fusion.5
  194.3 8.2 %attend_back.1 = (bf16[512,576]{1,0:T(8,128)(2,1)S(1)}, f32[3,1024]{1,0:T(4,128)S(1)}) custom-call(bf16[512,576]{1,0:T(8,128)(2,1)S(1)} %copy-done.1, bf16[512,192]{1,0:T(8,128)(2,1)S(1)} %copy.64.dmix_ref, f32[3,512,512]{2,1,0:T(8,128)S(1)} %get-tuple-element.35.probs_ref), custom_call_target="tpu_custom_call" | custom-call | tf_op jit(solution)/shard_map/attend_back/pallas_call | solution.py:217
  203.4 1.7 convolution_convert_fusion.2
  205.6 2.0 convolution_convert_fusion.1
  207.7 1.3 copy.66
  210.2 15.5 %exchange_6.1 = (bf16[4,128,768]{2,1,0:T(8,128)(2,1)}, bf16[4,192,192]{2,1,0:T(8,128)(2,1)}) custom-call(bf16[4,128,768]{2,1,0:T(8,128)(2,1)} %bitcast.80, bf16[4,192,192]{2,1,0:T(8,128)(2,1)} %bitcast.78), custom_call_target="tpu_custom_call" | custom-call | tf_op jit(solution)/shard_map/exchange_6/pallas_call | solution.py:129
  225.8 1.3 convert_reduce_fusion
  229.0 34.9 %exchange_7.1 = (bf16[8,96,576]{2,1,0:T(8,128)(2,1)}, bf16[8,96,192]{2,1,0:T(8,128)(2,1)}, f32[8,8,128]{2,1,0:T(8,128)}) custom-call(bf16[8,96,576]{2,1,0:T(8,128)(2,1)} %bitcast.74, bf16[8,96,192]{2,1,0:T(8,128)(2,1)} %bitcast.83, f32[8,8,128]{2,1,0:T(8,128)} %bitcast.84), custom_call_target="tpu_custom_call" | custom-call | tf_op jit(solution)/shard_map/exchange_7/pallas_call | solution.py:129
  263.9 1.4 reduce.1
  267.1 1.4 reduce_sum.208.refs_1_
  268.4 9.9 %exchange_8.1 = (bf16[4,96,768]{2,1,0:T(8,128)(2,1)}, f32[4,8,128]{2,1,0:T(8,128)}) custom-call(bf16[96,768]{1,0:T(8,128)(2,1)} %pad_maximum_fusion.1.refs_0_, f32[8,128]{1,0:T(8,128)} %reduce_sum.208.refs_1_), custom_call_target="tpu_custom_call" | custom-call | tf_op jit(solution)/shard_map/exchange_8/pallas_call | solution.py:129
  281.0 2.3 reshape.286
  283.3 1.3 fusion.140
  289.5 5.1 %fusion.45 = f32[576,3072]{1,0:T(8,128)S(1)} fusion(bf16[768,3072]{1,0:T(8,128)(2,1)} %param.27, bf16[576,1536]{1,0:T(8,128)(2,1)} %bitcast.98), kind=kOutput, calls=%fused_computation.66 | convolution fusion | flops 2717908992 | bytes 12681216 | tf_op jit(solution)/shard_map/dot_general | solution.py:28
  294.7 2.9 copy-done.36
  297.6 7.5 %fusion.7 = f32[3072,768]{1,0:T(8,128)} fusion(f32[576,3072]{1,0:T(8,128)S(1)} %fusion.45, bf16[576,1536]{1,0:T(8,128)(2,1)S(1)} %bitcast.99), kind=kOutput, calls=%fused_computation.10 | convolution fusion | flops 2733834240 | bytes 17399808 | tf_op jit(solution)/shard_map/dot_general | solution.py:32
  305.0 13.6 %fusion.12 = f32[768,3072]{1,0:T(8,128)} fusion(f32[576,3072]{1,0:T(8,128)} %copy-done.36, bf16[3072,768]{1,0:T(8,128)(2,1)} %param.28, bf16[576,1536]{1,0:T(8,128)(2,1)S(1)} %bitcast.100), kind=kOutput, calls=%fused_computation.15 | convolution fusion | flops 5471207424 | bytes 23003136 | tf_op jit(solution)/shard_map/dot_general | solution.py:32
  (144 shorter events, 34.4 us)
Async XLA Ops:
  2.7 3.4 %copy-start.27 = (pred[128]{0:T(512)(128)(4,1)}, pred[128]{0:T(512)(128)(4,1)S(1)}, u32[]{:S(2)}) copy-start(pred[128]{0:T(512)(128)(4,1)S(1)} %get-tuple-element.89) | copy-start | bytes 388
  2.7 76.0 %copy-start.18 = (f32[128]{0:T(128)}, f32[128]{0:T(128)S(1)}, u32[]{:S(2)}) copy-start(f32[128]{0:T(128)S(1)} %get-tuple-element.88) | copy-start | bytes 1540
  7.2 43.8 %copy-start.23 = (s32[1024]{0:T(1024)}, s32[1024]{0:T(1024)S(1)}, u32[]{:S(2)}) copy-start(s32[1024]{0:T(1024)S(1)} %pad_add_fusion) | copy-start | bytes 12292
  48.3 8.6 %copy-start.7 = (bf16[4,128,768]{2,1,0:T(8,128)(2,1)S(1)}, bf16[4,128,768]{2,1,0:T(8,128)(2,1)}, u32[]{:S(2)}) copy-start(bf16[4,128,768]{2,1,0:T(8,128)(2,1)} %get-tuple-element.29) | copy-start | bytes 2359300
  48.3 8.8 %copy-start.34 = (bf16[8,96,576]{2,1,0:T(8,128)(2,1)S(1)}, bf16[8,96,576]{2,1,0:T(8,128)(2,1)}, u32[]{:S(2)}) copy-start(bf16[8,96,576]{2,1,0:T(8,128)(2,1)} %get-tuple-element.31) | copy-start | bytes 2654212
  54.5 9.5 %copy-start.13 = (bf16[192,768]{1,0:T(8,128)(2,1)S(1)}, bf16[192,768]{1,0:T(8,128)(2,1)}, u32[]{:S(2)}) copy-start(bf16[192,768]{1,0:T(8,128)(2,1)} %reshape.265) | copy-start | bytes 884740
  62.5 0.8 copy-start
  63.3 0.7 copy-start.2
  63.3 17.9 %copy-start.15 = (bf16[768,8]{1,0:T(8,128)(2,1)S(1)}, bf16[768,8]{1,0:T(8,128)(2,1)}, u32[]{:S(2)}) copy-start(bf16[768,8]{1,0:T(8,128)(2,1)} %convert_element_type.143) | copy-start | bytes 36868
  63.3 19.5 %copy-start.9 = (bf16[128,768]{1,0:T(8,128)(2,1)S(1)}, bf16[128,768]{1,0:T(8,128)(2,1)}, u32[]{:S(2)}) copy-start(bf16[128,768]{1,0:T(8,128)(2,1)} %param.29) | copy-start | bytes 589828
  79.9 0.5 copy-start.29
  79.9 0.6 copy-start.31
  79.9 1.2 copy-start.5
  80.5 0.6 copy-start.20
  81.2 1.7 copy-start.12
  109.3 1.2 copy-start.14
  122.6 23.3 %copy-start.22 = (s32[128]{0:T(128)S(1)}, s32[128]{0:T(128)}, u32[]{:S(2)}) copy-start(s32[128]{0:T(128)} %add_select_fusion) | copy-start | bytes 1540
  122.6 23.3 %copy-start.25 = (s32[144]{0:T(256)S(1)}, s32[144]{0:T(256)}, u32[]{:S(2)}) copy-start(s32[144]{0:T(256)} %fusion.109) | copy-start | bytes 1732
  122.6 24.7 %copy-start.19 = (f32[128]{0:T(128)S(1)}, f32[128]{0:T(128)}, u32[]{:S(2)}) copy-start(f32[128]{0:T(128)} %copy-done.18) | copy-start | bytes 1540
  122.6 26.7 %copy-start.28 = (pred[128]{0:T(512)(128)(4,1)S(1)}, pred[128]{0:T(512)(128)(4,1)}, u32[]{:S(2)}) copy-start(pred[128]{0:T(512)(128)(4,1)} %copy-done.27) | copy-start | bytes 388
  122.7 26.7 %copy-start.17 = (s32[128,1]{0,1:T(1,128)S(1)}, s32[128,1]{0,1:T(1,128)}, u32[]{:S(2)}) copy-start(s32[128,1]{0,1:T(1,128)} %param.18) | copy-start | bytes 1540
  122.7 26.7 %copy-start.21 = (f32[128]{0:T(128)S(1)}, f32[128]{0:T(128)}, u32[]{:S(2)}) copy-start(f32[128]{0:T(128)} %copy-done.20) | copy-start | bytes 1540
  124.5 27.2 %copy-start.32 = (f32[128]{0:T(128)S(1)}, f32[128]{0:T(128)}, u32[]{:S(2)}) copy-start(f32[128]{0:T(128)} %copy-done.31) | copy-start | bytes 1540
  147.4 42.6 %copy-start.3 = (bf16[512,192]{1,0:T(8,128)(2,1)S(1)}, bf16[512,192]{1,0:T(8,128)(2,1)}, u32[]{:S(2)}) copy-start(bf16[512,192]{1,0:T(8,128)(2,1)} %copy-done.2) | copy-start | bytes 589828
  193.2 1.1 copy-start.1
  194.3 9.1 %copy-start.35 = (bf16[8,96,576]{2,1,0:T(8,128)(2,1)S(1)}, bf16[8,96,576]{2,1,0:T(8,128)(2,1)}, u32[]{:S(2)}) copy-start(bf16[8,96,576]{2,1,0:T(8,128)(2,1)} %get-tuple-element.31) | copy-start | bytes 2654212
  194.3 10.8 %copy-start.24 = (s32[1024]{0:T(1024)S(1)}, s32[1024]{0:T(1024)}, u32[]{:S(2)}) copy-start(s32[1024]{0:T(1024)} %copy-done.23) | copy-start | bytes 12292
  202.6 0.8 copy-start.4
  203.4 5.6 %copy-start.16 = (bf16[192,768]{1,0:T(8,128)(2,1)S(1)}, bf16[192,768]{1,0:T(8,128)(2,1)}, u32[]{:S(2)}) copy-start(bf16[192,768]{1,0:T(8,128)(2,1)} %convolution_convert_fusion.5) | copy-start | bytes 884740
  205.6 21.4 %copy-start.11 = (bf16[128,768]{1,0:T(8,128)(2,1)S(1)}, bf16[128,768]{1,0:T(8,128)(2,1)}, u32[]{:S(2)}) copy-start(bf16[128,768]{1,0:T(8,128)(2,1)} %refs_3_.1) | copy-start | bytes 589828
  205.6 21.4 %copy-start.26 = (f32[128]{0:T(128)S(1)}, f32[128]{0:T(128)}, u32[]{:S(2)}) copy-start(f32[128]{0:T(128)} %fusion.112) | copy-start | bytes 1540
  207.7 20.3 %copy-start.30 = (f32[128]{0:T(128)S(1)}, f32[128]{0:T(128)}, u32[]{:S(2)}) copy-start(f32[128]{0:T(128)} %copy-done.29) | copy-start | bytes 1540
  207.7 20.3 %copy-start.6 = (f32[128,768]{1,0:T(8,128)S(1)}, f32[128,768]{1,0:T(8,128)}, u32[]{:S(2)}) copy-start(f32[128,768]{1,0:T(8,128)} %copy-done.5) | copy-start | bytes 1179652
  207.7 20.3 %copy-start.8 = (f32[128,768]{1,0:T(8,128)S(1)}, f32[128,768]{1,0:T(8,128)}, u32[]{:S(2)}) copy-start(f32[128,768]{1,0:T(8,128)} %get-tuple-element.105) | copy-start | bytes 1179652
  207.7 20.3 %copy-start.10 = (bf16[128,768]{1,0:T(8,128)(2,1)S(1)}, bf16[128,768]{1,0:T(8,128)(2,1)}, u32[]{:S(2)}) copy-start(bf16[128,768]{1,0:T(8,128)(2,1)} %param.29) | copy-start | bytes 589828
  289.5 8.0 %copy-start.33 = (bf16[4,144,1536]{2,1,0:T(8,128)(2,1)S(1)}, bf16[4,144,1536]{2,1,0:T(8,128)(2,1)}, u32[]{:S(2)}) copy-start(bf16[4,144,1536]{2,1,0:T(8,128)(2,1)} %get-tuple-element.45) | copy-start | bytes 5308420
  294.7 2.9 copy-start.36

commit v2 on v1

--- a/solution.py
+++ b/solution.py
@@ -225,6 +225,189 @@
     )(qkv, dmix, probs)
 
 
+def closing_kernel(
+    sizes,
+    tile,
+    grads_ref,
+    small_ref,
+    got_ref,
+    w_in_ref,
+    w_out_ref,
+    weight_all_ref,
+    small_all_ref,
+    dw_in_ref,
+    dw_out_ref,
+    got_here,
+    w_in_here,
+    w_out_here,
+    dw_in_here,
+    dw_out_here,
+    land,
+    small_land,
+    piece,
+    small_piece,
+    load_sems,
+    store_sems,
+    own_sems,
+    dp_send,
+    dp_recv,
+    rep_send,
+    rep_recv,
+):
+    places = {axis: lax.axis_index(axis) for axis in ("dp", "rep")}
+    barrier = pltpu.get_barrier_semaphore()
+    for axis in ("dp", "rep"):
+        for step in range(1, sizes[axis]):
+            peer = lax.rem(places[axis] + step, sizes[axis])
+            pl.semaphore_signal(barrier, inc=1, device_id={axis: peer}, device_id_type=MESH)
+    dp_at, rep_at = places["dp"], places["rep"]
+    own = [
+        pltpu.make_async_copy(grads_ref.at[dp_at], land.at[dp_at], own_sems.at[0]),
+        pltpu.make_async_copy(small_ref.at[dp_at], small_land.at[dp_at], own_sems.at[1]),
+    ]
+    loads = [
+        pltpu.make_async_copy(got_ref, got_here, load_sems.at[0]),
+        pltpu.make_async_copy(w_in_ref, w_in_here, load_sems.at[1]),
+        pltpu.make_async_copy(w_out_ref, w_out_here, load_sems.at[2]),
+    ]
+    for copy in own + loads:
+        copy.start()
+    pl.semaphore_wait(barrier, sizes["dp"] + sizes["rep"] - 2)
+    across = []
+    for step in range(1, sizes["dp"]):
+        peer = lax.rem(dp_at + step, sizes["dp"])
+        for at, (from_ref, into_ref) in enumerate(((grads_ref, land), (small_ref, small_land))):
+            across.append(
+                pltpu.make_async_remote_copy(
+                    src_ref=from_ref.at[peer],
+                    dst_ref=into_ref.at[dp_at],
+                    send_sem=dp_send.at[at, step - 1],
+                    recv_sem=dp_recv.at[at, step - 1],
+                    device_id={"dp": peer},
+                    device_id_type=MESH,
+                )
+            )
+    for copy in across:
+        copy.start()
+    for copy in loads:
+        copy.wait()
+
+    model_width = w_in_ref.shape[0]
+    tiles = w_in_ref.shape[1] // tile
+
+    def stores(at):
+        here = pl.ds(pl.multiple_of(at * tile, tile), tile)
+        return (
+            pltpu.make_async_copy(
+                dw_in_here.at[:, here], dw_in_ref.at[:, here], store_sems.at[0, at]
+            ),
+            pltpu.make_async_copy(dw_out_here.at[here], dw_out_ref.at[here], store_sems.at[1, at]),
+        )
+
+    def one_tile(at, carry):
+        here = pl.ds(pl.multiple_of(at * tile, tile), tile)
+        rows, grads = got_here[:, :model_width], got_here[:, model_width:]
+        pre = matmul(rows, w_in_here[:, here])
+        squared = pre * pre
+        bent = jnp.tanh(0.7978845608028654 * pre * (1.0 + 0.044715 * squared))
+        half = 0.5 * (1.0 + bent)
+        slope = half + 0.5 * pre * (1.0 - bent * bent) * (
+            0.7978845608028654 * (1.0 + 3.0 * 0.044715 * squared)
+        )
+        act = (pre * half).astype(jnp.bfloat16)
+        dpre = (dot_over(grads, w_out_here[here, :], 1, 1) * slope).astype(jnp.bfloat16)
+        dw_in_here[:, here] = dot_over(rows, dpre, 0, 0).astype(jnp.bfloat16)
+        dw_out_here[here, :] = dot_over(act, grads, 0, 0).astype(jnp.bfloat16)
+        for copy in stores(at):
+            copy.start()
+        return carry
+
+    early = tiles - tiles // 4
+    lax.fori_loop(0, early, one_tile, 0)
+    for copy in own + across:
+        copy.wait()
+    total = land[0].astype(jnp.float32)
+    small_total = small_land[0]
+    for at in range(1, sizes["dp"]):
+        total = total + land[at].astype(jnp.float32)
+        small_total = small_total + small_land[at]
+    piece[...] = total.astype(jnp.bfloat16)
+    small_piece[...] = small_total
+    last = [
+        pltpu.make_async_copy(piece, weight_all_ref.at[rep_at], own_sems.at[2]),
+        pltpu.make_async_copy(small_piece, small_all_ref.at[rep_at], own_sems.at[3]),
+    ]
+    for step in range(1, sizes["rep"]):
+        peer = lax.rem(rep_at + step, sizes["rep"])
+        for at, (from_ref, into_ref) in enumerate(
+            ((piece, weight_all_ref), (small_piece, small_all_ref))
+        ):
+            last.append(
+                pltpu.make_async_remote_copy(
+                    src_ref=from_ref,
+                    dst_ref=into_ref.at[rep_at],
+                    send_sem=rep_send.at[at, step - 1],
+                    recv_sem=rep_recv.at[at, step - 1],
+                    device_id={"rep": peer},
+                    device_id_type=MESH,
+                )
+            )
+    for copy in last:
+        copy.start()
+    lax.fori_loop(early, tiles, one_tile, 0)
+
+    def finish(at, carry):
+        for copy in stores(at):
+            copy.wait()
+        return carry
+
+    lax.fori_loop(0, tiles, finish, 0)
+    for copy in last:
+        copy.wait()
+
+
+def closing(mark, grads, small, got, w_in, w_out):
+    sizes = {"dp": lax.axis_size("dp"), "rep": lax.axis_size("rep")}
+    hidden = w_in.shape[1]
+    tile = 256 if hidden % 256 == 0 else 128
+    rest = pl.BlockSpec(memory_space=pl.ANY)
+    low_type = jnp.bfloat16
+    dma = pltpu.SemaphoreType.DMA
+    return pl.pallas_call(
+        functools.partial(closing_kernel, sizes, tile),
+        out_shape=(
+            jax.ShapeDtypeStruct((sizes["rep"],) + grads.shape[1:], low_type),
+            jax.ShapeDtypeStruct((sizes["rep"],) + small.shape[1:], jnp.float32),
+            jax.ShapeDtypeStruct(w_in.shape, low_type),
+            jax.ShapeDtypeStruct(w_out.shape, low_type),
+        ),
+        in_specs=[rest] * 5,
+        out_specs=(rest,) * 4,
+        scratch_shapes=[
+            pltpu.VMEM(got.shape, low_type),
+            pltpu.VMEM(w_in.shape, low_type),
+            pltpu.VMEM(w_out.shape, low_type),
+            pltpu.VMEM(w_in.shape, low_type),
+            pltpu.VMEM(w_out.shape, low_type),
+            pltpu.VMEM(grads.shape, low_type),
+            pltpu.VMEM(small.shape, jnp.float32),
+            pltpu.VMEM(grads.shape[1:], low_type),
+            pltpu.VMEM(small.shape[1:], jnp.float32),
+            dma((3,)),
+            dma((2, hidden // tile)),
+            dma((4,)),
+            dma((2, sizes["dp"] - 1)),
+            dma((2, sizes["dp"] - 1)),
+            dma((2, sizes["rep"] - 1)),
+            dma((2, sizes["rep"] - 1)),
+        ],
+        compiler_params=pltpu.CompilerParams(
+            collective_id=mark, has_side_effects=True, vmem_limit_bytes=VMEM_LIMIT
+        ),
+        name="closing",
+    )(grads, small, got, w_in, w_out)
+
+
 def packed(parts, lead):
     flat = jnp.concatenate([piece.reshape(lead + (-1,)) for piece in parts], axis=-1)
     count = flat.shape[-1]
@@ -376,8 +559,11 @@
         [matmul(act_here, w_out).astype(low_type), dot_over(dpre_here, w_in, 1, 1).astype(low_type)],
         axis=1,
     )
-    (returned,) = exchange(
-        4, (("dp", "swap", 0),), back.reshape(dp_count, capacity, 2 * model_width)
+    returned, got_all = exchange(
+        4,
+        (("dp", "swap", 0), ("rep", "gather", 1)),
+        back.reshape(dp_count, capacity, 2 * model_width),
+        got,
     )
     landed = dot_over(dispatch, returned.reshape(dp_count * capacity, 2 * model_width), 0, 0)
     expert_rows, grad_h_two = landed[:, :model_width], landed[:, model_width:]
@@ -397,9 +583,7 @@
     grad_x_one = grad_out + grad_x_norm
     grad_branch = (grad_x_one * row_live).astype(low_type)
 
-    branch_all, got_all = exchange(
-        5, (("rep", "gather", 0), ("rep", "gather", 1)), grad_branch, got
-    )
+    (branch_all,) = exchange(5, (("rep", "gather", 0),), grad_branch)
     grad_branch_group = branch_all.reshape(group_rows, model_width)
     grad_w_output = dot_over(mixture, grad_branch_group, 0, 0).astype(low_type)
     dmix = dot_over(grad_branch_group, w_out_rows, 1, 1).astype(low_type)
@@ -428,25 +612,19 @@
         ],
         (dp_count,),
     )
-    weight_got, out_got, small_got = exchange(
+    weight_all, small_all, grad_w_in, grad_w_out = closing(
         7,
-        (("dp", "swap", 0), ("dp", "swap", 1), ("dp", "swap", 2)),
-        grad_w_qkv.reshape(dp_count, shard, 3 * width),
-        grad_out_cols.reshape(dp_count, shard, width),
+        jnp.concatenate(
+            [
+                grad_w_qkv.reshape(dp_count, shard, 3 * width),
+                grad_out_cols.reshape(dp_count, shard, width),
+            ],
+            axis=2,
+        ),
         small_grads,
-    )
-    weight_sum = jnp.concatenate(
-        [
-            jnp.sum(weight_got.astype(jnp.float32), axis=0),
-            jnp.sum(out_got.astype(jnp.float32), axis=0),
-        ],
-        axis=1,
-    ).astype(low_type)
-    weight_all, small_all = exchange(
-        8,
-        (("rep", "gather", 0), ("rep", "gather", 1)),
-        weight_sum,
-        jnp.sum(small_got, axis=0),
+        got_all.reshape(-1, 2 * model_width),
+        w_in,
+        w_out,
     )
     weights = (
         weight_all.reshape(rep_count, shard, 4, width)
@@ -457,11 +635,6 @@
     small_sum = jnp.sum(small_all, axis=0).reshape(-1)
     out_gain_one, out_gain_two, out_table, out_router = unpacked(small_sum, small_widths)
 
-    got_all = got_all.reshape(-1, 2 * model_width)
-    rows_all, grads_all = got_all[:, :model_width], got_all[:, model_width:]
-    act_all, dpre_all = expert(rows_all, grads_all)
-    grad_w_in = dot_over(rows_all, dpre_all, 0, 0)
-    grad_w_out = dot_over(act_all, grads_all, 0, 0)
     return (
         block_out.astype(low_type),
         grad_input,
@@ -473,8 +646,8 @@
         out_table,
         out_gain_two,
         out_router.reshape(shard, EXPERTS),
-        grad_w_in,
-        grad_w_out,
+        grad_w_in.astype(jnp.float32),
+        grad_w_out.astype(jnp.float32),
     )
 
 

time: 322 us -> 281 us (0.87)
  matrix products: 60.7 us -> 33.8 us
  Pallas kernels: 186 us -> 167 us
  other arithmetic: 27.6 us -> 38.3 us
    pallas_call x8 -> x6, Pallas kernels: 173 us -> 114 us  [exchange(): pl.pallas_call(functools.partial(exchange_kernel, jobs, sizes, len(arrays...]
    pallas_call x0 -> x1, Pallas kernels: none -> 39.5 us  [closing(): pl.pallas_call(functools.partial(closing_kernel, sizes, tile), out_shape=...]
    dot_general x8 -> x6, matrix products: 39.3 us -> 18 us  [dot_over(): lax.dot_general(left_op, right_op, (((left_dim,), (right_dim,)), ((), ())...]
    convert_element_type x0 -> x2, other arithmetic: none -> 12 us  [the longest x1 7.52 us: on_device(): grad_w_in.astype(jnp.float32)]
    dot_general x8 -> x7, matrix products: 16.8 us -> 11.7 us  [matmul(): return jnp.dot(left_op, right_op, preferred_element_type=jnp.float32)]
    reduce_sum x3 -> x0, other arithmetic: 3.78 us -> none  [the longest x1 1.36 us: on_device(): jnp.sum(small_got, axis=0)]
    unnamed x80 -> x88, local copies, waits for them, and re-layouts: 11.4 us -> 8.65 us
where the time goes in v2:
time: 281 us; the launch traced here: 280 us
  Pallas kernels  167 us (59%)
  local copies, waits for them, and re-layouts  39.9 us (14%)
  other arithmetic  38.3 us (14%)
  matrix products  33.8 us (12%)
    pallas_call x6, Pallas kernels, exchange(): pl.pallas_call(functools.partial(exchange_kernel, jobs, sizes, len(arrays...  114 us
    pallas_call x1, Pallas kernels, closing(): pl.pallas_call(functools.partial(closing_kernel, sizes, tile), out_shape=...  39.5 us
    dot_general x6, matrix products, dot_over(): lax.dot_general(left_op, right_op, (((left_dim,), (right_dim,)), ((), ())...  18 us
    dot_general x7, matrix products, matmul(): return jnp.dot(left_op, right_op, preferred_element_type=jnp.float32)  11.7 us
    unnamed x88, local copies, waits for them, and re-layouts  8.65 us
    pallas_call x1, Pallas kernels, attend_back(): pl.pallas_call(functools.partial(attend_back_kernel, heads, block), out_s...  8.23 us
    convert_element_type x1, other arithmetic, on_device(): grad_w_in.astype(jnp.float32)  7.52 us

profile of v2, /device:TPU:13, one launch (start us, length us, event | category | flops | bytes accessed | tf_op | source)
XLA Modules:
  0.0 279.9 jit_solution(1199139292303663422)
XLA Ops:
  3.6 1.2 add_select_fusion
  8.1 1.4 fusion.70.refs_2_
  10.5 1.6 constant_dynamic-slice_fusion
  13.0 35.4 %exchange_1.1 = (bf16[8,96,576]{2,1,0:T(8,128)(2,1)}, bf16[8,96,192]{2,1,0:T(8,128)(2,1)}, f32[8,8,128]{2,1,0:T(8,128)}, bf16[4,128,768]{2,1,0:T(8,128)(2,1)}, bf16[4,2,96,192]{3,2,1,0:T(8,128)(2,1)}) custom-call(bf16[96,576]{1,0:T(8,128)(2,1)} %pad_maximum_fusion.2.refs_0_, bf16[96,192]{1,0:T(8,128)(2,1)} %get-tuple-element.104.refs_1_, ...), custom_call_target="tpu_custom_call" | custom-call | tf_op jit(solution)/shard_map/exchange_1/pallas_call | solution.py:129
  49.2 1.4 multiply_reduce_fusion
  52.1 1.3 copy.82
  53.4 1.1 reshape.265
  54.5 1.1 fusion.8
  56.7 4.5 %attend.1 = (f32[3,512,512]{2,1,0:T(8,128)S(1)}, bf16[512,192]{1,0:T(8,128)(2,1)S(1)}) custom-call(bf16[512,576]{1,0:T(8,128)(2,1)S(1)} %convolution_convert_fusion.4.qkv_ref, f32[3,1024]{1,0:T(4,128)S(1)} %fusion.42.line_ref, s32[512,1]{1,0:T(8,128)S(1)} %copy.62.seg_col_ref, s32[1,512]{1,0:T(1,128)S(1)} %bitcast.72), custom_call_target="tpu_custom_call" | custom-call | tf_op jit(solution)/shard_map/attend/pallas_call | solution.py:167
  62.8 1.2 convolution_convert_fusion.3
  64.0 12.2 %exchange_2.1 = bf16[4,128,768]{2,1,0:T(8,128)(2,1)} custom-call(bf16[4,128,768]{2,1,0:T(8,128)(2,1)} %bitcast.79), custom_call_target="tpu_custom_call" | custom-call | tf_op jit(solution)/shard_map/exchange_2/pallas_call | solution.py:129
  76.3 1.4 convert_reduce_fusion.1
  77.7 1.1 multiply_reduce_fusion.3
  81.3 1.1 convolution_convert_fusion
  82.4 2.0 reshape.267.refs_0_
  84.4 17.4 %exchange_3.1 = bf16[8,18,1536]{2,1,0:T(8,128)(2,1)} custom-call(bf16[8,18,1536]{2,1,0:T(8,128)(2,1)} %reshape.267.refs_0_), custom_call_target="tpu_custom_call" | custom-call | tf_op jit(solution)/shard_map/exchange_3/pallas_call | solution.py:129
  101.8 2.0 reshape.268.refs_1_
  103.8 3.3 %fusion.39 = f32[144,3072]{1,0:T(8,128)S(1)} fusion(bf16[768,3072]{1,0:T(8,128)(2,1)} %w_in_ref.1, bf16[144,1536]{1,0:T(8,128)(2,1)} %reshape.268.refs_1_), kind=kOutput, calls=%fused_computation.73 | convolution fusion | flops 679477248 | bytes 6709248 | tf_op jit(solution)/shard_map/dot_general | solution.py:28
  107.1 1.2 copy-done.15
  108.3 4.2 %convolution_convert_fusion.7 = bf16[144,768]{1,0:T(8,128)(2,1)} fusion(bf16[3072,768]{1,0:T(8,128)(2,1)} %w_out_ref.1, f32[144,3072]{1,0:T(8,128)S(1)} %fusion.39), kind=kOutput, calls=%fused_computation.25 | convolution fusion | flops 683569152 | bytes 6709248 | tf_op jit(solution)/shard_map/dot_general | solution.py:28
  112.5 8.6 %convolution_convert_fusion.6 = bf16[144,768]{1,0:T(8,128)(2,1)} fusion(bf16[768,3072]{1,0:T(8,128)(2,1)} %w_in_ref.1, f32[144,3072]{1,0:T(8,128)} %copy-done.15, bf16[3072,768]{1,0:T(8,128)(2,1)} %w_out_ref.1, bf16[144,1536]{1,0:T(8,128)(2,1)} %reshape.268.refs_1_), kind=kOutput, calls=%fused_computation.24 | convolution fusion | flops 1367912448 | bytes 11649024 | tf_op jit(solution)/shard_map/dot_general | solution.py:32
  121.1 1.8 pad_maximum_fusion.1
  123.0 2.0 reshape.269.refs_0_
  124.9 22.7 %exchange_4.1 = (bf16[8,18,1536]{2,1,0:T(8,128)(2,1)}, bf16[4,144,1536]{2,1,0:T(8,128)(2,1)}) custom-call(bf16[8,18,1536]{2,1,0:T(8,128)(2,1)} %reshape.269.refs_0_, bf16[144,1536]{1,0:T(8,128)(2,1)} %reshape.268.refs_1_), custom_call_target="tpu_custom_call" | custom-call | tf_op jit(solution)/shard_map/exchange_4/pallas_call | solution.py:129
  147.6 2.0 reshape.270
  149.6 1.4 fusion.43
  151.0 1.8 fusion.24
  154.2 2.5 multiply_reduce_fusion.1
  157.1 1.3 reshape.277
  158.5 1.3 fusion.63
  160.7 2.1 multiply_convert_fusion.3.refs_0_
  162.7 11.3 %exchange_5.1 = bf16[4,128,768]{2,1,0:T(8,128)(2,1)} custom-call(bf16[128,768]{1,0:T(8,128)(2,1)} %multiply_convert_fusion.3.refs_0_), custom_call_target="tpu_custom_call" | custom-call | tf_op jit(solution)/shard_map/exchange_5/pallas_call | solution.py:129
  174.0 2.3 convolution_convert_fusion.8
  176.3 2.2 convolution_convert_fusion.5
  178.5 1.1 copy.64.dmix_ref
  179.6 1.1 copy-done.1
  180.6 8.2 %attend_back.1 = (bf16[512,576]{1,0:T(8,128)(2,1)S(1)}, f32[3,1024]{1,0:T(4,128)S(1)}) custom-call(bf16[512,576]{1,0:T(8,128)(2,1)S(1)} %copy-done.1, bf16[512,192]{1,0:T(8,128)(2,1)S(1)} %copy.64.dmix_ref, f32[3,512,512]{2,1,0:T(8,128)S(1)} %get-tuple-element.34.probs_ref), custom_call_target="tpu_custom_call" | custom-call | tf_op jit(solution)/shard_map/attend_back/pallas_call | solution.py:217
  189.7 1.7 convolution_convert_fusion.2
  191.9 1.8 convolution_convert_fusion.1
  195.6 15.5 %exchange_6.1 = (bf16[4,128,768]{2,1,0:T(8,128)(2,1)}, bf16[4,192,192]{2,1,0:T(8,128)(2,1)}) custom-call(bf16[4,128,768]{2,1,0:T(8,128)(2,1)} %bitcast.82, bf16[4,192,192]{2,1,0:T(8,128)(2,1)} %bitcast.80), custom_call_target="tpu_custom_call" | custom-call | tf_op jit(solution)/shard_map/exchange_6/pallas_call | solution.py:129
  211.1 1.3 convert_reduce_fusion
  212.5 1.4 pad_maximum_fusion.grads_ref
  216.8 2.2 fusion.25
  219.0 39.5 %closing.1 = (bf16[4,96,768]{2,1,0:T(8,128)(2,1)S(1)}, f32[4,8,128]{2,1,0:T(8,128)S(1)}, bf16[768,3072]{1,0:T(8,128)(2,1)}, bf16[3072,768]{1,0:T(8,128)(2,1)}) custom-call(bf16[8,96,768]{2,1,0:T(8,128)(2,1)S(1)} %pad_maximum_fusion.grads_ref, f32[8,8,128]{2,1,0:T(8,128)S(1)} %bitcast.70, bf16[576,1536]{1,0:T(8,128)(2,1)S(1)} %bitcast.69, ...), custom_call_target="tpu_custom_call" | custom-call | tf_op jit(solution)/shard_map/closing/pallas_call | solution.py:376
  260.5 1.1 reshape.286
  261.6 1.3 fusion.106
  267.9 7.5 %convert_element_type.158 = f32[768,3072]{1,0:T(8,128)} convert(bf16[768,3072]{1,0:T(8,128)(2,1)} %get-tuple-element.42) | non-fusion elementwise | flops 2359296 | bytes 14155776 | tf_op jit(solution)/shard_map/convert_element_type | solution.py:649
  275.4 4.5 %convert_element_type.159 = f32[3072,768]{1,0:T(8,128)} convert(bf16[3072,768]{1,0:T(8,128)(2,1)S(1)} %bitcast.77) | non-fusion elementwise | flops 2359296 | bytes 14155776 | tf_op jit(solution)/shard_map/convert_element_type | solution.py:650
  (148 shorter events, 31.0 us)
Async XLA Ops:
  2.7 3.4 %copy-start.32 = (pred[128]{0:T(512)(128)(4,1)}, pred[128]{0:T(512)(128)(4,1)S(1)}, u32[]{:S(2)}) copy-start(pred[128]{0:T(512)(128)(4,1)S(1)} %get-tuple-element.87) | copy-start | bytes 388
  2.7 75.0 %copy-start.22 = (f32[128]{0:T(128)}, f32[128]{0:T(128)S(1)}, u32[]{:S(2)}) copy-start(f32[128]{0:T(128)S(1)} %get-tuple-element.86) | copy-start | bytes 1540
  7.2 43.7 %copy-start.27 = (s32[1024]{0:T(1024)}, s32[1024]{0:T(1024)S(1)}, u32[]{:S(2)}) copy-start(s32[1024]{0:T(1024)S(1)} %pad_add_fusion) | copy-start | bytes 12292
  48.3 6.2 %copy-start.8 = (bf16[4,128,768]{2,1,0:T(8,128)(2,1)S(1)}, bf16[4,128,768]{2,1,0:T(8,128)(2,1)}, u32[]{:S(2)}) copy-start(bf16[4,128,768]{2,1,0:T(8,128)(2,1)} %get-tuple-element.28) | copy-start | bytes 2359300
  53.4 2.5 copy-start.37
  55.9 6.9 %copy-start.14 = (bf16[192,768]{1,0:T(8,128)(2,1)S(1)}, bf16[192,768]{1,0:T(8,128)(2,1)}, u32[]{:S(2)}) copy-start(bf16[192,768]{1,0:T(8,128)(2,1)} %reshape.265) | copy-start | bytes 884740
  61.2 0.8 copy-start
  62.1 0.7 copy-start.3
  76.2 3.9 %copy-start.16 = (bf16[768,8]{1,0:T(8,128)(2,1)S(1)}, bf16[768,8]{1,0:T(8,128)(2,1)}, u32[]{:S(2)}) copy-start(bf16[768,8]{1,0:T(8,128)(2,1)} %convert_element_type.136) | copy-start | bytes 36868
  76.2 4.1 %copy-start.21 = (s32[128,1]{0,1:T(1,128)S(1)}, s32[128,1]{0,1:T(1,128)}, u32[]{:S(2)}) copy-start(s32[128,1]{0,1:T(1,128)} %param.18) | copy-start | bytes 1540
  76.2 4.6 %copy-start.33 = (pred[128]{0:T(512)(128)(4,1)S(1)}, pred[128]{0:T(512)(128)(4,1)}, u32[]{:S(2)}) copy-start(pred[128]{0:T(512)(128)(4,1)} %copy-done.32) | copy-start | bytes 388
  76.2 4.6 %copy-start.10 = (bf16[128,768]{1,0:T(8,128)(2,1)S(1)}, bf16[128,768]{1,0:T(8,128)(2,1)}, u32[]{:S(2)}) copy-start(bf16[128,768]{1,0:T(8,128)(2,1)} %param.29) | copy-start | bytes 589828
  76.2 5.1 %copy-start.24 = (s32[128]{0:T(128)S(1)}, s32[128]{0:T(128)}, u32[]{:S(2)}) copy-start(s32[128]{0:T(128)} %add_select_fusion) | copy-start | bytes 1540
  76.3 5.1 %copy-start.29 = (s32[144]{0:T(256)S(1)}, s32[144]{0:T(256)}, u32[]{:S(2)}) copy-start(s32[144]{0:T(256)} %fusion.85) | copy-start | bytes 1732
  78.8 0.6 copy-start.34
  78.8 0.6 copy-start.35
  78.9 75.3 %copy-start.6 = (f32[128,768]{1,0:T(8,128)}, f32[128,768]{1,0:T(8,128)S(1)}, u32[]{:S(2)}) copy-start(f32[128,768]{1,0:T(8,128)S(1)} %get-tuple-element.85) | copy-start | bytes 1179652
  79.4 0.5 copy-start.23
  80.1 0.9 copy-start.13
  80.3 0.5 copy-start.20
  80.8 0.5 copy-start.30
  107.1 1.2 copy-start.15
  149.6 4.6 %copy-start.17 = (bf16[768,8]{1,0:T(8,128)(2,1)S(1)}, bf16[768,8]{1,0:T(8,128)(2,1)}, u32[]{:S(2)}) copy-start(bf16[768,8]{1,0:T(8,128)(2,1)} %convert_element_type.136) | copy-start | bytes 36868
  149.6 7.0 %copy-start.36 = (f32[128]{0:T(128)S(1)}, f32[128]{0:T(128)}, u32[]{:S(2)}) copy-start(f32[128]{0:T(128)} %copy-done.35) | copy-start | bytes 1540
  153.4 3.2 %copy-start.25 = (f32[128]{0:T(128)}, f32[128]{0:T(128)S(1)}, u32[]{:S(2)}) copy-start(f32[128]{0:T(128)S(1)} %broadcast_select_fusion) | copy-start | bytes 1540
  154.1 2.5 copy-start.26
  160.6 15.6 %copy-start.4 = (bf16[512,192]{1,0:T(8,128)(2,1)S(1)}, bf16[512,192]{1,0:T(8,128)(2,1)}, u32[]{:S(2)}) copy-start(bf16[512,192]{1,0:T(8,128)(2,1)} %copy-done.3) | copy-start | bytes 589828
  179.6 1.1 copy-start.1
  180.6 9.1 %copy-start.38 = (bf16[8,96,576]{2,1,0:T(8,128)(2,1)S(1)}, bf16[8,96,576]{2,1,0:T(8,128)(2,1)}, u32[]{:S(2)}) copy-start(bf16[8,96,576]{2,1,0:T(8,128)(2,1)} %get-tuple-element.30) | copy-start | bytes 2654212
  188.9 0.8 copy-start.5
  188.9 2.5 copy-start.28
  188.9 3.0 %copy-start.19 = (bf16[512,768]{1,0:T(8,128)(2,1)S(1)}, bf16[512,768]{1,0:T(8,128)(2,1)}, u32[]{:S(2)}) copy-start(bf16[512,768]{1,0:T(8,128)(2,1)} %fusion.8) | copy-start | bytes 2359300
  191.9 2.5 copy-start.18
  211.1 2.8 copy-start.12
  211.1 2.8 copy-start.31
  212.5 1.4 copy-start.9
  212.5 4.3 %copy-start.7 = (f32[128,768]{1,0:T(8,128)S(1)}, f32[128,768]{1,0:T(8,128)}, u32[]{:S(2)}) copy-start(f32[128,768]{1,0:T(8,128)} %copy-done.6) | copy-start | bytes 1179652
  212.5 4.3 %copy-start.11 = (bf16[128,768]{1,0:T(8,128)(2,1)S(1)}, bf16[128,768]{1,0:T(8,128)(2,1)}, u32[]{:S(2)}) copy-start(bf16[128,768]{1,0:T(8,128)(2,1)} %param.29) | copy-start | bytes 589828
  213.9 5.1 %copy-start.2 = (bf16[4,144,1536]{2,1,0:T(8,128)(2,1)S(1)}, bf16[4,144,1536]{2,1,0:T(8,128)(2,1)}, u32[]{:S(2)}) copy-start(bf16[4,144,1536]{2,1,0:T(8,128)(2,1)} %get-tuple-element.39) | copy-start | bytes 5308420
  266.9 8.5 %slice-start = ((s8[4718592]{0:T(1024)(128)(4,1)}), s8[524288]{0:T(1024)(128)(4,1)S(1)}, s32[]{:S(2)}) async-start(s8[4718592]{0:T(1024)(128)(4,1)} %bitcast.76), calls=%async_computation | async-start | bytes 1048576
  267.9 7.5 %slice-start.1 = ((s8[4718592]{0:T(1024)(128)(4,1)}), s8[4194304]{0:T(1024)(128)(4,1)S(1)}, s32[]{:S(2)}) async-start(s8[4718592]{0:T(1024)(128)(4,1)} %bitcast.76), calls=%async_computation.1 | async-start | bytes 8388608

commit v3 on v2

--- a/solution.py
+++ b/solution.py
@@ -58,7 +58,7 @@
         send, recv, own = sems[3 * at : 3 * at + 3]
 
         def part(peer):
-            if kind == "gather":
+            if kind in ("gather", "relay"):
                 return from_ref
             if kind == "swap":
                 return from_ref.at[peer]
@@ -67,6 +67,24 @@
 
         if not with_remote:
             return [pltpu.make_async_copy(part(me), into_ref.at[me], own)]
+        if kind == "relay":
+            across, beside = lax.rem(me + 2, count), me + 1 - 2 * lax.rem(me, 2)
+            hops = (
+                (from_ref, me, across),
+                (from_ref, me, beside),
+                (into_ref.at[across], across, beside),
+            )
+            return [
+                pltpu.make_async_remote_copy(
+                    src_ref=source_ref,
+                    dst_ref=into_ref.at[slot],
+                    send_sem=send.at[hop],
+                    recv_sem=recv.at[hop],
+                    device_id={axis: peer},
+                    device_id_type=MESH,
+                )
+                for hop, (source_ref, slot, peer) in enumerate(hops)
+            ]
         found = []
         for step in range(1, count):
             peer = lax.rem(me + step, count)
@@ -92,9 +110,14 @@
     first.sort(key=lambda at: not any(jobs[other][2] == ("out", at) for other in later))
     for at in first:
         more = local_and_remote(at, True)
-        for copy in more:
+        for copy in more[: 2 if jobs[at][1] == "relay" else None]:
             copy.start()
         flying[at] += more
+    for at in first:
+        if jobs[at][1] == "relay":
+            flying[at][1].wait()
+            flying[at][3].start()
+            del flying[at][1]
     for at in later:
         for copy in flying.pop(jobs[at][2][1]):
             copy.wait()
@@ -112,7 +135,7 @@
     for axis, kind, source in jobs:
         like = shapes[source[1]] if isinstance(source, tuple) else arrays[source]
         count = sizes[axis]
-        if kind == "gather":
+        if kind in ("gather", "relay"):
             shape = (count,) + tuple(like.shape)
         elif kind == "swap":
             shape = tuple(like.shape)
@@ -223,6 +246,55 @@
         compiler_params=pltpu.CompilerParams(vmem_limit_bytes=VMEM_LIMIT),
         name="attend_back",
     )(qkv, dmix, probs)
+
+
+def gelu_and_slope(pre):
+    squared = pre * pre
+    bent = jnp.tanh(0.7978845608028654 * pre * (1.0 + 0.044715 * squared))
+    half = 0.5 * (1.0 + bent)
+    slope = half + 0.5 * pre * (1.0 - bent * bent) * (
+        0.7978845608028654 * (1.0 + 3.0 * 0.044715 * squared)
+    )
+    return pre * half, slope
+
+
+def expert_kernel(got_ref, w_in_ref, w_out_ref, back_ref, total):
+    step = pl.program_id(0)
+    model_width = w_in_ref.shape[0]
+    rows, grads = got_ref[:, :model_width], got_ref[:, model_width:]
+    act, slope = gelu_and_slope(matmul(rows, w_in_ref[...]))
+    dpre = (dot_over(grads, w_out_ref[...], 1, 1) * slope).astype(jnp.bfloat16)
+
+    @pl.when(step == 0)
+    def _():
+        total[...] = jnp.zeros_like(total)
+
+    total[:, :model_width] += matmul(act.astype(jnp.bfloat16), w_out_ref[...])
+    total[:, model_width:] += dot_over(dpre, w_in_ref[...], 1, 1)
+
+    @pl.when(step == pl.num_programs(0) - 1)
+    def _():
+        back_ref[...] = total[...].astype(jnp.bfloat16)
+
+
+def expert_rows_both_ways(got, w_in, w_out):
+    model_width, hidden = w_in.shape
+    tile = 512 if hidden % 512 == 0 else 128
+    whole = pl.BlockSpec(got.shape, lambda step: (0, 0))
+    return pl.pallas_call(
+        expert_kernel,
+        grid=(hidden // tile,),
+        out_shape=jax.ShapeDtypeStruct(got.shape, jnp.bfloat16),
+        in_specs=[
+            whole,
+            pl.BlockSpec((model_width, tile), lambda step: (0, step)),
+            pl.BlockSpec((tile, model_width), lambda step: (step, 0)),
+        ],
+        out_specs=whole,
+        scratch_shapes=[pltpu.VMEM(got.shape, jnp.float32)],
+        compiler_params=pltpu.CompilerParams(vmem_limit_bytes=VMEM_LIMIT),
+        name="expert_rows",
+    )(got, w_in, w_out)
 
 
 def closing_kernel(
@@ -308,13 +380,8 @@
         here = pl.ds(pl.multiple_of(at * tile, tile), tile)
         rows, grads = got_here[:, :model_width], got_here[:, model_width:]
         pre = matmul(rows, w_in_here[:, here])
-        squared = pre * pre
-        bent = jnp.tanh(0.7978845608028654 * pre * (1.0 + 0.044715 * squared))
-        half = 0.5 * (1.0 + bent)
-        slope = half + 0.5 * pre * (1.0 - bent * bent) * (
-            0.7978845608028654 * (1.0 + 3.0 * 0.044715 * squared)
-        )
-        act = (pre * half).astype(jnp.bfloat16)
+        act, slope = gelu_and_slope(pre)
+        act = act.astype(jnp.bfloat16)
         dpre = (dot_over(grads, w_out_here[here, :], 1, 1) * slope).astype(jnp.bfloat16)
         dw_in_here[:, here] = dot_over(rows, dpre, 0, 0).astype(jnp.bfloat16)
         dw_out_here[here, :] = dot_over(act, grads, 0, 0).astype(jnp.bfloat16)
@@ -456,6 +523,7 @@
     width = heads * HEAD
     shard = w_query.shape[0]
     low_type = jnp.bfloat16
+    spread_kind = "relay" if rep_count == 4 else "gather"
 
     piece_qkv = jnp.concatenate(
         [local_columns(full, width, rep_at) for full in (w_query, w_key, w_value)], axis=1
@@ -546,22 +614,10 @@
         3, (("dp", "swap", 0),), sent.reshape(dp_count, capacity, 2 * model_width)
     )
     got = got.reshape(dp_count * capacity, 2 * model_width)
-    rows_here, grads_here = got[:, :model_width], got[:, model_width:]
-
-    def expert(rows, grads):
-        pre = matmul(rows, w_in)
-        act, pull = jax.vjp(lambda inner: jax.nn.gelu(inner, approximate=True), pre)
-        dpre = pull(dot_over(grads, w_out, 1, 1))[0]
-        return act.astype(low_type), dpre.astype(low_type)
-
-    act_here, dpre_here = expert(rows_here, grads_here)
-    back = jnp.concatenate(
-        [matmul(act_here, w_out).astype(low_type), dot_over(dpre_here, w_in, 1, 1).astype(low_type)],
-        axis=1,
-    )
+    back = expert_rows_both_ways(got, w_in, w_out)
     returned, got_all = exchange(
         4,
-        (("dp", "swap", 0), ("rep", "gather", 1)),
+        (("dp", "swap", 0), ("rep", spread_kind, 1)),
         back.reshape(dp_count, capacity, 2 * model_width),
         got,
     )
@@ -583,7 +639,7 @@
     grad_x_one = grad_out + grad_x_norm
     grad_branch = (grad_x_one * row_live).astype(low_type)
 
-    (branch_all,) = exchange(5, (("rep", "gather", 0),), grad_branch)
+    (branch_all,) = exchange(5, (("rep", spread_kind, 0),), grad_branch)
     grad_branch_group = branch_all.reshape(group_rows, model_width)
     grad_w_output = dot_over(mixture, grad_branch_group, 0, 0).astype(low_type)
     dmix = dot_over(grad_branch_group, w_out_rows, 1, 1).astype(low_type)

time: 281 us -> 248 us (0.88)
  matrix products: 33.8 us -> 12.9 us
  other arithmetic: 38.3 us -> 30.5 us
  local copies, waits for them, and re-layouts: 39.9 us -> 34.1 us
    dot_general x6 -> x5, matrix products: 18 us -> 8.37 us  [dot_over(): lax.dot_general(left_op, right_op, (((left_dim,), (right_dim,)), ((), ())...]
    pallas_call x0 -> x1, Pallas kernels: none -> 8.53 us  [expert_rows_both_ways(): pl.pallas_call(expert_kernel, grid=(hidden // tile,), out_shape=jax.Shape...]
    dot_general x7 -> x5, matrix products: 11.7 us -> 3.38 us  [matmul(): return jnp.dot(left_op, right_op, preferred_element_type=jnp.float32)]
    pallas_call x6, Pallas kernels: 114 us -> 107 us  [exchange(): pl.pallas_call(functools.partial(exchange_kernel, jobs, sizes, len(arrays...]
    unnamed x88 -> x64, local copies, waits for them, and re-layouts: 8.65 us -> 8.68 us
where the time goes in v3:
time: 248 us; the launch traced here: 247 us
  Pallas kernels  168 us (68%)
  local copies, waits for them, and re-layouts  34.1 us (14%)
  other arithmetic  30.5 us (12%)
  matrix products  12.9 us (5%)
    pallas_call x6, Pallas kernels, exchange(): pl.pallas_call(functools.partial(exchange_kernel, jobs, sizes, len(arrays...  107 us
    pallas_call x1, Pallas kernels, closing(): pl.pallas_call(functools.partial(closing_kernel, sizes, tile), out_shape=...  39 us
    unnamed x64, local copies, waits for them, and re-layouts  8.68 us
    pallas_call x1, Pallas kernels, expert_rows_both_ways(): pl.pallas_call(expert_kernel, grid=(hidden // tile,), out_shape=jax.Shape...  8.53 us
    dot_general x5, matrix products, dot_over(): lax.dot_general(left_op, right_op, (((left_dim,), (right_dim,)), ((), ())...  8.37 us
    pallas_call x1, Pallas kernels, attend_back(): pl.pallas_call(functools.partial(attend_back_kernel, heads, block), out_s...  8.25 us
    convert_element_type x1, other arithmetic, on_device(): grad_w_in.astype(jnp.float32)  7.52 us

profile of v3, /device:TPU:13, one launch (start us, length us, event | category | flops | bytes accessed | tf_op | source)
XLA Modules:
  0.0 246.6 jit_solution(9004299206435012892)
XLA Ops:
  0.6 0.8 reduce-window.4
  2.7 0.9 fusion.4
  7.0 1.4 fusion.44.refs_2_
  8.3 1.0 constant_dynamic-slice_fusion.2
  9.4 1.6 constant_dynamic-slice_fusion
  11.9 35.4 %exchange_1.1 = (bf16[8,96,576]{2,1,0:T(8,128)(2,1)}, bf16[8,96,192]{2,1,0:T(8,128)(2,1)}, f32[8,8,128]{2,1,0:T(8,128)}, bf16[4,128,768]{2,1,0:T(8,128)(2,1)}, bf16[4,2,96,192]{3,2,1,0:T(8,128)(2,1)}) custom-call(bf16[96,576]{1,0:T(8,128)(2,1)} %pad_maximum_fusion.1.refs_0_, bf16[96,192]{1,0:T(8,128)(2,1)} %get-tuple-element.104.refs_1_, ...), custom_call_target="tpu_custom_call" | custom-call | tf_op jit(solution)/shard_map/exchange_1/pallas_call | solution.py:152
  47.3 0.8 copy.84
  48.1 1.4 multiply_reduce_fusion
  50.4 1.3 copy.82
  52.1 1.1 fusion.1
  54.4 4.6 %attend.1 = (f32[3,512,512]{2,1,0:T(8,128)S(1)}, bf16[512,192]{1,0:T(8,128)(2,1)S(1)}) custom-call(bf16[512,576]{1,0:T(8,128)(2,1)S(1)} %convolution_convert_fusion.4.qkv_ref, f32[3,1024]{1,0:T(4,128)S(1)} %fusion.16.line_ref, s32[512,1]{1,0:T(8,128)S(1)} %copy.62.seg_col_ref, s32[1,512]{1,0:T(1,128)S(1)} %bitcast.68), custom_call_target="tpu_custom_call" | custom-call | tf_op jit(solution)/shard_map/attend/pallas_call | solution.py:190
  59.0 1.7 copy-done.2
  60.7 1.2 convolution_convert_fusion.3
  61.9 12.2 %exchange_2.1 = bf16[4,128,768]{2,1,0:T(8,128)(2,1)} custom-call(bf16[4,128,768]{2,1,0:T(8,128)(2,1)} %bitcast.75), custom_call_target="tpu_custom_call" | custom-call | tf_op jit(solution)/shard_map/exchange_2/pallas_call | solution.py:152
  74.1 1.3 convert_reduce_fusion.1
  77.2 0.9 reshape.267.refs_0_
  78.1 17.4 %exchange_3.1 = bf16[8,18,1536]{2,1,0:T(8,128)(2,1)} custom-call(bf16[8,18,1536]{2,1,0:T(8,128)(2,1)} %reshape.267.refs_0_), custom_call_target="tpu_custom_call" | custom-call | tf_op jit(solution)/shard_map/exchange_3/pallas_call | solution.py:152
  95.5 1.2 reshape.268.got_ref.refs_1_
  96.7 2.3 copy-done
  99.1 8.5 %expert_rows.1 = bf16[144,1536]{1,0:T(8,128)(2,1)S(1)} custom-call(bf16[144,1536]{1,0:T(8,128)(2,1)S(1)} %reshape.268.got_ref.refs_1_, bf16[768,3072]{1,0:T(8,128)(2,1)S(1)} %copy-done, bf16[3072,768]{1,0:T(8,128)(2,1)} %w_out_ref.3), custom_call_target="tpu_custom_call" | custom-call | tf_op jit(solution)/shard_map/expert_rows/pallas_call | solution.py:284
  107.6 0.9 reshape.269.refs_0_
  108.6 17.6 %exchange_4.1 = (bf16[8,18,1536]{2,1,0:T(8,128)(2,1)}, bf16[4,144,1536]{2,1,0:T(8,128)(2,1)}) custom-call(bf16[8,18,1536]{2,1,0:T(8,128)(2,1)} %reshape.269.refs_0_, bf16[144,1536]{1,0:T(8,128)(2,1)} %copy-done.1), custom_call_target="tpu_custom_call" | custom-call | tf_op jit(solution)/shard_map/exchange_4/pallas_call | solution.py:152
  126.2 1.2 reshape.270
  130.3 0.8 reshape.279
  131.1 0.9 multiply_convert_fusion.1.refs_0_
  132.0 9.4 %exchange_5.1 = bf16[4,128,768]{2,1,0:T(8,128)(2,1)} custom-call(bf16[128,768]{1,0:T(8,128)(2,1)} %multiply_convert_fusion.1.refs_0_), custom_call_target="tpu_custom_call" | custom-call | tf_op jit(solution)/shard_map/exchange_5/pallas_call | solution.py:152
  141.3 2.3 convolution_convert_fusion.6
  143.6 2.2 convolution_convert_fusion.5
  145.8 1.1 copy.64.dmix_ref
  146.9 1.1 copy-done.5
  148.0 8.3 %attend_back.1 = (bf16[512,576]{1,0:T(8,128)(2,1)S(1)}, f32[3,1024]{1,0:T(4,128)S(1)}) custom-call(bf16[512,576]{1,0:T(8,128)(2,1)S(1)} %copy-done.5, bf16[512,192]{1,0:T(8,128)(2,1)S(1)} %copy.64.dmix_ref, f32[3,512,512]{2,1,0:T(8,128)S(1)} %copy-done.3), custom_call_target="tpu_custom_call" | custom-call | tf_op jit(solution)/shard_map/attend_back/pallas_call | solution.py:240
  156.3 0.8 copy-done.7
  157.1 1.7 convolution_convert_fusion.2
  159.1 1.8 convolution_convert_fusion.1
  162.8 15.6 %exchange_6.1 = (bf16[4,128,768]{2,1,0:T(8,128)(2,1)}, bf16[4,192,192]{2,1,0:T(8,128)(2,1)}) custom-call(bf16[4,128,768]{2,1,0:T(8,128)(2,1)} %bitcast.78, bf16[4,192,192]{2,1,0:T(8,128)(2,1)} %bitcast.76), custom_call_target="tpu_custom_call" | custom-call | tf_op jit(solution)/shard_map/exchange_6/pallas_call | solution.py:152
  178.3 1.3 convert_reduce_fusion
  179.7 1.4 pad_maximum_fusion.grads_ref
  182.5 0.8 fusion.26
  184.0 2.2 fusion.7
  186.3 39.0 %closing.1 = (bf16[4,96,768]{2,1,0:T(8,128)(2,1)S(1)}, f32[4,8,128]{2,1,0:T(8,128)S(1)}, bf16[768,3072]{1,0:T(8,128)(2,1)}, bf16[3072,768]{1,0:T(8,128)(2,1)}) custom-call(bf16[8,96,768]{2,1,0:T(8,128)(2,1)S(1)} %pad_maximum_fusion.grads_ref, f32[8,8,128]{2,1,0:T(8,128)S(1)} %bitcast.66, bf16[576,1536]{1,0:T(8,128)(2,1)S(1)} %bitcast.65, ...), custom_call_target="tpu_custom_call" | custom-call | tf_op jit(solution)/shard_map/closing/pallas_call | solution.py:443
  227.2 1.1 reshape.286
  228.4 1.3 fusion.70
  230.0 1.0 squeeze.21
  231.2 1.0 squeeze.20
  232.4 1.0 squeeze.19
  233.7 1.0 squeeze.18
  234.6 7.5 %convert_element_type.142 = f32[768,3072]{1,0:T(8,128)} convert(bf16[768,3072]{1,0:T(8,128)(2,1)} %get-tuple-element.42) | non-fusion elementwise | flops 2359296 | bytes 14155776 | tf_op jit(solution)/shard_map/convert_element_type | solution.py:705
  242.2 4.5 %convert_element_type.143 = f32[3072,768]{1,0:T(8,128)} convert(bf16[3072,768]{1,0:T(8,128)(2,1)S(1)} %bitcast.73) | non-fusion elementwise | flops 2359296 | bytes 14155776 | tf_op jit(solution)/shard_map/convert_element_type | solution.py:706
  (121 shorter events, 19.5 us)
Async XLA Ops:
  47.3 4.8 %copy-start.10 = (bf16[4,128,768]{2,1,0:T(8,128)(2,1)S(1)}, bf16[4,128,768]{2,1,0:T(8,128)(2,1)}, u32[]{:S(2)}) copy-start(bf16[4,128,768]{2,1,0:T(8,128)(2,1)} %get-tuple-element.28) | copy-start | bytes 2359300
  52.0 8.7 %copy-start.17 = (bf16[192,768]{1,0:T(8,128)(2,1)}, bf16[192,768]{1,0:T(8,128)(2,1)S(1)}, u32[]{:S(2)}) copy-start(bf16[192,768]{1,0:T(8,128)(2,1)S(1)} %reshape.265) | copy-start | bytes 884740
  52.0 1.6 copy-start.25
  54.4 4.6 %copy-start.4 = (bf16[512,576]{1,0:T(8,128)(2,1)}, bf16[512,576]{1,0:T(8,128)(2,1)S(1)}, u32[]{:S(2)}) copy-start(bf16[512,576]{1,0:T(8,128)(2,1)S(1)} %convolution_convert_fusion.4.qkv_ref) | copy-start | bytes 1769476
  59.0 1.7 copy-start.2
  61.9 13.6 %copy-start.15 = (bf16[128,768]{1,0:T(8,128)(2,1)S(1)}, bf16[128,768]{1,0:T(8,128)(2,1)}, u32[]{:S(2)}) copy-start(bf16[128,768]{1,0:T(8,128)(2,1)} %refs_3_.1) | copy-start | bytes 589828
  74.1 2.6 %copy-start.20 = (s32[128,1]{0,1:T(1,128)S(1)}, s32[128,1]{0,1:T(1,128)}, u32[]{:S(2)}) copy-start(s32[128,1]{0,1:T(1,128)} %param.18) | copy-start | bytes 1540
  74.1 2.6 %copy-start.13 = (bf16[128,768]{1,0:T(8,128)(2,1)S(1)}, bf16[128,768]{1,0:T(8,128)(2,1)}, u32[]{:S(2)}) copy-start(bf16[128,768]{1,0:T(8,128)(2,1)} %param.29) | copy-start | bytes 589828
  75.7 0.9 copy-start.24
  75.7 55.4 %copy-start.8 = (f32[128,768]{1,0:T(8,128)}, f32[128,768]{1,0:T(8,128)S(1)}, u32[]{:S(2)}) copy-start(f32[128,768]{1,0:T(8,128)S(1)} %get-tuple-element.85) | copy-start | bytes 1179652
  75.7 55.4 %copy-start.21 = (f32[128]{0:T(128)}, f32[128]{0:T(128)S(1)}, u32[]{:S(2)}) copy-start(f32[128]{0:T(128)S(1)} %fusion.61) | copy-start | bytes 1540
  96.7 2.3 copy-start
  99.1 8.5 %copy-start.1 = (bf16[144,1536]{1,0:T(8,128)(2,1)}, bf16[144,1536]{1,0:T(8,128)(2,1)S(1)}, u32[]{:S(2)}) copy-start(bf16[144,1536]{1,0:T(8,128)(2,1)S(1)} %reshape.268.got_ref.refs_1_) | copy-start | bytes 1327108
  129.1 1.9 copy-start.11
  129.2 1.9 copy-start.22
  131.9 14.9 %copy-start.3 = (f32[3,512,512]{2,1,0:T(8,128)S(1)}, f32[3,512,512]{2,1,0:T(8,128)}, u32[]{:S(2)}) copy-start(f32[3,512,512]{2,1,0:T(8,128)} %copy-done.2) | copy-start | bytes 9437188
  146.9 1.1 copy-start.5
  148.0 9.1 %copy-start.26 = (bf16[8,96,576]{2,1,0:T(8,128)(2,1)S(1)}, bf16[8,96,576]{2,1,0:T(8,128)(2,1)}, u32[]{:S(2)}) copy-start(bf16[8,96,576]{2,1,0:T(8,128)(2,1)} %get-tuple-element.30) | copy-start | bytes 2654212
  156.3 0.8 copy-start.7
  156.3 2.9 %copy-start.19 = (bf16[512,768]{1,0:T(8,128)(2,1)S(1)}, bf16[512,768]{1,0:T(8,128)(2,1)}, u32[]{:S(2)}) copy-start(bf16[512,768]{1,0:T(8,128)(2,1)} %fusion.1) | copy-start | bytes 2359300
  159.1 2.5 copy-start.18
  179.6 2.2 copy-start.12
  179.6 1.5 copy-start.16
  179.6 1.5 copy-start.23
  179.7 4.4 %copy-start.9 = (f32[128,768]{1,0:T(8,128)S(1)}, f32[128,768]{1,0:T(8,128)}, u32[]{:S(2)}) copy-start(f32[128,768]{1,0:T(8,128)} %copy-done.8) | copy-start | bytes 1179652
  179.7 4.4 %copy-start.14 = (bf16[128,768]{1,0:T(8,128)(2,1)S(1)}, bf16[128,768]{1,0:T(8,128)(2,1)}, u32[]{:S(2)}) copy-start(bf16[128,768]{1,0:T(8,128)(2,1)} %param.29) | copy-start | bytes 589828
  181.1 5.1 %copy-start.6 = (bf16[4,144,1536]{2,1,0:T(8,128)(2,1)S(1)}, bf16[4,144,1536]{2,1,0:T(8,128)(2,1)}, u32[]{:S(2)}) copy-start(bf16[4,144,1536]{2,1,0:T(8,128)(2,1)} %get-tuple-element.39) | copy-start | bytes 5308420
  233.6 8.5 %slice-start = ((s8[4718592]{0:T(1024)(128)(4,1)}), s8[524288]{0:T(1024)(128)(4,1)S(1)}, s32[]{:S(2)}) async-start(s8[4718592]{0:T(1024)(128)(4,1)} %bitcast.72), calls=%async_computation | async-start | bytes 1048576
  234.6 7.5 %slice-start.1 = ((s8[4718592]{0:T(1024)(128)(4,1)}), s8[4194304]{0:T(1024)(128)(4,1)S(1)}, s32[]{:S(2)}) async-start(s8[4718592]{0:T(1024)(128)(4,1)} %bitcast.72), calls=%async_computation.1 | async-start | bytes 8388608
